TPU v7x, 512 devices: a whole 4x8x8 slice. The times are simulated.
512 devices in a mesh: seq: 128 (over y, z, core), head: 4 (over x).
Axes of the slice: x: 4, y: 8, z: 8, core: 2. Of those that a mesh axis runs over, the one named last changes fastest.
Arguments:
- queries: bfloat16 [32768, 1024], P('seq', 'head'), may hold values from -8 to 8
- key_rows: bfloat16 [32768, 1024], P('seq', 'head'), may hold values from -8 to 8
- value_rows: bfloat16 [32768, 1024], P('seq', 'head'), may hold values from -6 to 6
- attn_out_grad: bfloat16 [32768, 1024], P('seq', 'head'), may hold values from -6 to 6
- ssm_input: bfloat16 [32768, 512], P('seq', 'head'), may hold values from -6 to 6
- b_matrix: bfloat16 [32768, 256], P('seq'), may hold values from -2 to 2
- c_matrix: bfloat16 [32768, 256], P('seq'), may hold values from -2 to 2
- step_sizes: float32 [32768, 8], P('seq', 'head'), may hold values from 0.005 to 0.05
- decay_rates: float32 [8], P('head'), may hold values from 1.5258789e-05 to 0.5
- skip_gain: float32 [8], P('head'), may hold values from 0.5 to 1.5
- ssm_out_grad: bfloat16 [32768, 512], P('seq', 'head'), may hold values from -6 to 6
- doc_lengths: int32 [128], replicated, may hold values from 1 to 512, 32768 in all
Outputs:
- attn_out: bfloat16 [32768, 1024], P('seq', 'head')
- query_grad: bfloat16 [32768, 1024], P('seq', 'head')
- key_grad: bfloat16 [32768, 1024], P('seq', 'head')
- value_grad: bfloat16 [32768, 1024], P('seq', 'head')
- ssm_out: bfloat16 [32768, 512], P('seq', 'head')
- input_grad: bfloat16 [32768, 512], P('seq', 'head')
- b_grad: float32 [32768, 256], P('seq')
- c_grad: float32 [32768, 256], P('seq')
All inputs are finite; a program needn't handle non-finite values.
Results may differ from a plain program's by a relative error of at most 0.022.
Values may be sent and summed in bfloat16 or wider, within the bound.
A program may use at most 128 MiB of HBM per device.

v0:
```python
import jax
import jax.numpy as jnp
from jax import lax
from jax.sharding import Mesh
from jax.sharding import PartitionSpec as P

HEAD_DIM = 128
REACH = 2
SEQ = ("seq_0", "seq_1", "seq_2")


def shifted(x, axis, by):
    length = lax.axis_size(axis)
    pairs = [(i, i + by) for i in range(length) if 0 <= i + by < length]
    return lax.ppermute(x, axis, pairs)


def filled_with(x, identity):
    return jax.tree.map(
        lambda part, zero: jnp.zeros_like(part) + jnp.asarray(zero, part.dtype), x, identity
    )


def carried_in(x, axes, combine, identity, reverse):
    before = start = filled_with(x, identity)
    subtotal = x
    for axis in reversed(axes):
        length, index = (lax.axis_size(axis), lax.axis_index(axis))
        pieces = jax.tree.map(lambda part: lax.all_gather(part, axis), subtotal)
        inside, subtotal = (start, start)
        for k in reversed(range(length)) if reverse else range(length):
            passed = k > index if reverse else k < index
            subtotal = combine(subtotal, jax.tree.map(lambda part: part[k], pieces))
            inside = jax.tree.map(lambda new, old: jnp.where(passed, new, old), subtotal, inside)
        before = combine(inside, before)
    return before


def from_everyone(x, axis):
    copies = jnp.broadcast_to(x, (lax.axis_size(axis), *x.shape))
    return lax.all_to_all(copies, axis, split_axis=0, concat_axis=0, tiled=True)


def taken_together(x, axis):
    return from_everyone(x, axis).sum(axis=0)


def doc_index(positions, doc_ends):
    return jnp.sum((positions[:, None] >= doc_ends[None, :]).astype(jnp.int32), axis=1)


def visible_mask(query_pos, key_pos, doc_ends):
    same_doc = doc_index(query_pos, doc_ends)[:, None] == doc_index(key_pos, doc_ends)[None, :]
    return same_doc & (key_pos[None, :] <= query_pos[:, None]) & (key_pos[None, :] >= 0)


def split_heads(block_rows, head_width):
    return block_rows.reshape(block_rows.shape[0], -1, head_width)


def tile_reaches(query_first, key_last, doc_starts):
    opening = jnp.max(jnp.where(doc_starts <= query_first, doc_starts, 0))
    return opening <= key_last


def run_tile(reaches, work, running):
    return lax.cond(reaches, work, lambda unchanged: unchanged, running)


def scores_of(query_heads, key_heads, tile_mask):
    scores = jnp.einsum(
        "thd,shd->hts", query_heads, key_heads, preferred_element_type=jnp.float32
    ) * HEAD_DIM ** (-0.5)
    return jnp.where(tile_mask[None], scores, -jnp.inf)


def probabilities(scores, tile_mask, row_top, row_total):
    return jnp.where(
        tile_mask[None], jnp.exp(scores - row_top[:, :, None]) / row_total[:, :, None], 0.0
    )


def tile_slopes(
    query_heads, key_heads, value_heads, grad_heads, tile_mask, row_top, row_total, row_delta
):
    tile_probs = probabilities(
        scores_of(query_heads, key_heads, tile_mask), tile_mask, row_top, row_total
    )
    prob_grad = jnp.einsum(
        "thd,shd->hts", grad_heads, value_heads, preferred_element_type=jnp.float32
    )
    dscore = (tile_probs * (prob_grad - row_delta[:, :, None]) * HEAD_DIM ** (-0.5)).astype(
        jnp.bfloat16
    )
    return (tile_probs.astype(jnp.bfloat16), dscore)


def attention(queries, key_rows, value_rows, attn_out_grad, doc_ends, doc_starts):
    row_count = queries.shape[0]
    query_pos = lax.axis_index(SEQ) * row_count + jnp.arange(row_count, dtype=jnp.int32)
    query_heads = split_heads(queries, HEAD_DIM)
    grad_heads = split_heads(attn_out_grad, HEAD_DIM)
    key_heads = split_heads(key_rows, HEAD_DIM)
    value_heads = split_heads(value_rows, HEAD_DIM)
    head_count = query_heads.shape[1]
    blocks = [(key_heads, value_heads, query_pos)]
    for distance in range(1, REACH + 1):
        far_keys, far_values = shifted((key_rows, value_rows), SEQ, distance)
        blocks.append(
            (
                split_heads(far_keys, HEAD_DIM),
                split_heads(far_values, HEAD_DIM),
                query_pos - distance * row_count,
            )
        )
    tile_masks = [visible_mask(query_pos, entry[2], doc_ends) for entry in blocks]
    reaches = [tile_reaches(query_pos[0], entry[2][-1], doc_starts) for entry in blocks]
    softmax_stats = (
        jnp.full((head_count, row_count), -jnp.inf, jnp.float32),
        jnp.zeros((head_count, row_count), jnp.float32),
    )
    for tile_index in range(len(blocks)):

        def grow_stats(running, key_block=blocks[tile_index][0], tile_mask=tile_masks[tile_index]):
            row_top, row_total = running
            scores = scores_of(query_heads, key_block, tile_mask)
            new_top = jnp.maximum(row_top, jnp.max(scores, axis=-1))
            new_total = row_total * jnp.exp(row_top - new_top) + jnp.sum(
                jnp.exp(scores - new_top[:, :, None]), axis=-1
            )
            return (new_top, new_total)

        if tile_index == 0:
            softmax_stats = grow_stats(softmax_stats)
        else:
            softmax_stats = run_tile(reaches[tile_index], grow_stats, softmax_stats)
    row_top, row_total = softmax_stats
    weighted = jnp.zeros((row_count, head_count, HEAD_DIM), jnp.float32)
    for tile_index in range(len(blocks)):

        def spread(running, key_block=blocks[tile_index], tile_mask=tile_masks[tile_index]):
            tile_probs = probabilities(
                scores_of(query_heads, key_block[0], tile_mask), tile_mask, row_top, row_total
            ).astype(jnp.bfloat16)
            return running + jnp.einsum(
                "hts,shd->thd", tile_probs, key_block[1], preferred_element_type=jnp.float32
            )

        if tile_index == 0:
            weighted = spread(weighted)
        else:
            weighted = run_tile(reaches[tile_index], spread, weighted)
    attn_rows = weighted.astype(jnp.bfloat16)
    row_delta = jnp.sum(grad_heads.astype(jnp.float32) * attn_rows.astype(jnp.float32), axis=-1).T
    probs_low, dscore = tile_slopes(
        query_heads,
        key_heads,
        value_heads,
        grad_heads,
        tile_masks[0],
        row_top,
        row_total,
        row_delta,
    )
    query_acc = jnp.einsum("hts,shd->thd", dscore, key_heads, preferred_element_type=jnp.float32)
    key_acc = jnp.einsum("hts,thd->shd", dscore, query_heads, preferred_element_type=jnp.float32)
    value_acc = jnp.einsum(
        "hts,thd->shd", probs_low, grad_heads, preferred_element_type=jnp.float32
    )
    zero_keys = jnp.zeros((row_count, head_count, HEAD_DIM), jnp.float32)
    for tile_index in range(1, len(blocks)):

        def slope_tile(running, key_block=blocks[tile_index], tile_mask=tile_masks[tile_index]):
            tile_low, tile_dscore = tile_slopes(
                query_heads,
                key_block[0],
                key_block[1],
                grad_heads,
                tile_mask,
                row_top,
                row_total,
                row_delta,
            )
            query_part = running[0] + jnp.einsum(
                "hts,shd->thd", tile_dscore, key_block[0], preferred_element_type=jnp.float32
            )
            key_part = jnp.einsum(
                "hts,thd->shd", tile_dscore, query_heads, preferred_element_type=jnp.float32
            )
            value_part = jnp.einsum(
                "hts,thd->shd", tile_low, grad_heads, preferred_element_type=jnp.float32
            )
            return (query_part, key_part, value_part)

        query_acc, key_part, value_part = run_tile(
            reaches[tile_index], slope_tile, (query_acc, zero_keys, zero_keys)
        )
        back_keys, back_values = shifted((key_part, value_part), SEQ, -tile_index)
        key_acc = key_acc + back_keys
        value_acc = value_acc + back_values
    return (
        attn_rows.reshape(row_count, -1),
        query_acc.astype(jnp.bfloat16).reshape(row_count, -1),
        key_acc.astype(jnp.bfloat16).reshape(row_count, -1),
        value_acc.astype(jnp.bfloat16).reshape(row_count, -1),
    )


def ssm_parts(x_heads, b_rows, intersection, step_sizes, decay_rates, skip_gain):
    row_count = x_heads.shape[0]
    offsets = jnp.arange(row_count, dtype=jnp.int32)
    log_decay = jnp.cumsum(-step_sizes * decay_rates[None, :], axis=0)
    causal = offsets[None, :] <= offsets[:, None]
    log_gaps = log_decay.T[:, :, None] - log_decay.T[:, None, :]
    fading = jnp.where(causal[None], jnp.exp(jnp.where(causal[None], log_gaps, 0.0)), 0.0)
    mixing = intersection[None] * fading * step_sizes.T[:, None, :]
    direct = jnp.einsum("hts,shp->thp", mixing, x_heads, precision=lax.Precision.HIGHEST)
    direct = direct + skip_gain[None, :, None] * x_heads
    carry_weight = jnp.exp(log_decay)
    tail_weight = jnp.exp(log_decay[-1][None, :] - log_decay) * step_sizes
    local_state = jnp.einsum(
        "th,tn,thp->hnp", tail_weight, b_rows, x_heads, precision=lax.Precision.HIGHEST
    )
    decay_all = jnp.exp(log_decay[-1])
    return (direct, local_state, decay_all, carry_weight)


def chained(earlier, later_item):
    return (earlier[0] * later_item[0], later_item[0][:, None, None] * earlier[1] + later_item[1])


def ssm_layer(ssm_input, b_matrix, c_matrix, step_sizes, decay_rates, skip_gain, ssm_out_grad):
    row_count = ssm_input.shape[0]
    head_count = decay_rates.shape[0]
    x_heads = ssm_input.astype(jnp.float32).reshape(row_count, head_count, -1)
    b_rows = b_matrix.astype(jnp.float32)
    c_rows = c_matrix.astype(jnp.float32)
    intersection = jnp.dot(c_matrix, b_matrix.T, preferred_element_type=jnp.float32)

    def local_terms(x_value, b_value, intersection_value):
        return ssm_parts(x_value, b_value, intersection_value, step_sizes, decay_rates, skip_gain)

    (direct, local_state, decay_all, carry_weight), pullback = jax.vjp(
        local_terms, x_heads, b_rows, intersection
    )
    identity = (jnp.ones_like(decay_all), jnp.zeros_like(local_state))
    state_in = carried_in((decay_all, local_state), SEQ, chained, identity, False)[1]
    incoming = jnp.einsum("tn,hnp->thp", c_rows, state_in, precision=lax.Precision.HIGHEST)
    ssm_rows = direct + carry_weight[:, :, None] * incoming
    grad_heads = ssm_out_grad.astype(jnp.float32).reshape(row_count, head_count, -1)
    adjoint = jnp.einsum(
        "th,tn,thp->hnp", carry_weight, c_rows, grad_heads, precision=lax.Precision.HIGHEST
    )
    adjoint_in = carried_in((decay_all, adjoint), SEQ, chained, identity, True)[1]
    weight_grad = jnp.sum(grad_heads * incoming, axis=-1)
    x_grad, b_grad, intersection_grad = pullback(
        (grad_heads, adjoint_in, jnp.zeros_like(decay_all), weight_grad)
    )
    b_grad = b_grad + jnp.dot(intersection_grad.T, c_rows, precision=lax.Precision.HIGHEST)
    c_grad = jnp.dot(intersection_grad, b_rows, precision=lax.Precision.HIGHEST)
    c_grad = c_grad + jnp.einsum(
        "th,thp,hnp->tn", carry_weight, grad_heads, state_in, precision=lax.Precision.HIGHEST
    )
    b_grad, c_grad = (taken_together(b_grad, "head"), taken_together(c_grad, "head"))
    return (
        ssm_rows.reshape(row_count, -1).astype(jnp.bfloat16),
        x_grad.reshape(row_count, -1).astype(jnp.bfloat16),
        b_grad,
        c_grad,
    )


def on_device(
    queries,
    key_rows,
    value_rows,
    attn_out_grad,
    ssm_input,
    b_matrix,
    c_matrix,
    step_sizes,
    decay_rates,
    skip_gain,
    ssm_out_grad,
    doc_lengths,
):
    doc_ends = jnp.cumsum(doc_lengths, dtype=jnp.int32)
    doc_starts = doc_ends - doc_lengths
    attn_out, query_grad, key_grad, value_grad = attention(
        queries, key_rows, value_rows, attn_out_grad, doc_ends, doc_starts
    )
    ssm_out, input_grad, b_grad, c_grad = ssm_layer(
        ssm_input, b_matrix, c_matrix, step_sizes, decay_rates, skip_gain, ssm_out_grad
    )
    return (attn_out, query_grad, key_grad, value_grad, ssm_out, input_grad, b_grad, c_grad)


def solution(mesh):
    split = Mesh(
        mesh.devices.reshape(8, 8, 2, mesh.shape["head"]), ("seq_0", "seq_1", "seq_2", "head")
    )
    return jax.shard_map(
        on_device,
        mesh=split,
        in_specs=(
            P(SEQ, "head"),
            P(SEQ, "head"),
            P(SEQ, "head"),
            P(SEQ, "head"),
            P(SEQ, "head"),
            P(SEQ, None),
            P(SEQ, None),
            P(SEQ, "head"),
            P("head"),
            P("head"),
            P(SEQ, "head"),
            P(),
        ),
        out_specs=(
            P(SEQ, "head"),
            P(SEQ, "head"),
            P(SEQ, "head"),
            P(SEQ, "head"),
            P(SEQ, "head"),
            P(SEQ, "head"),
            P(SEQ, None),
            P(SEQ, None),
        ),
        check_vma=False,
    )
```

profile of v0, /device:TPU:8, one launch (start us, length us, event | category | flops | bytes accessed | tf_op | source)
XLA Modules:
  0.0 215.3 jit_solution(4916960675997001807)
XLA Ops:
  7.2 0.8 multiply_bitcast_fusion
  9.6 1.8 all-gather.2
  11.4 0.6 copy-done.43
  12.2 0.9 copy.235
  13.4 2.0 all-gather.1
  15.4 0.7 bitcast_add_fusion.8
  16.2 0.8 copy-done.8
  17.1 2.2 %collective-permute-start = (bf16[256,256]{0,1:T(8,128)(2,1)S(1)}, bf16[256,256]{0,1:T(8,128)(2,1)S(1)}, u32[]{:S(2)}, u32[]{:S(2)}) collective-permute-start(bf16[256,256]{0,1:T(8,128)(2,1)S(1)} %copy.192), channel_id=1, source_target_pairs={{0,4},{4,8},{8,12},{12,16},{16,20},{20,24},{24,28},{28,32},{32,36}... | collective-permute-start | bytes 393224 | tf_op jit(solution)/shard_map/ppermute | solution.py:15
  19.4 4.3 %collective-permute-start.1 = (bf16[256,256]{0,1:T(8,128)(2,1)S(1)}, bf16[256,256]{0,1:T(8,128)(2,1)S(1)}, u32[]{:S(2)}, u32[]{:S(2)}) collective-permute-start(bf16[256,256]{0,1:T(8,128)(2,1)S(1)} %copy.192), channel_id=1, source_target_pairs={{0,8},{4,12},{8,16},{12,20},{16,24},{20,28},{24,32},{28,36},{32,40... | collective-permute-start | bytes 393224 | tf_op jit(solution)/shard_map/ppermute | solution.py:15
  23.8 4.0 %collective-permute-start.2 = (bf16[256,256]{0,1:T(8,128)(2,1)S(1)}, bf16[256,256]{0,1:T(8,128)(2,1)}, u32[]{:S(2)}, u32[]{:S(2)}) collective-permute-start(bf16[256,256]{0,1:T(8,128)(2,1)S(1)} %copy.202), channel_id=1, source_target_pairs={{0,4},{4,8},{8,12},{12,16},{16,20},{20,24},{24,28},{28,32},{32,36}... | collective-permute-start | bytes 393224 | tf_op jit(solution)/shard_map/ppermute | solution.py:15
  27.8 4.3 %collective-permute-start.3 = (bf16[256,256]{0,1:T(8,128)(2,1)S(1)}, bf16[256,256]{0,1:T(8,128)(2,1)}, u32[]{:S(2)}, u32[]{:S(2)}) collective-permute-start(bf16[256,256]{0,1:T(8,128)(2,1)S(1)} %copy.202), channel_id=1, source_target_pairs={{0,8},{4,12},{8,16},{12,20},{16,24},{20,28},{24,32},{28,36},{32,40... | collective-permute-start | bytes 393224 | tf_op jit(solution)/shard_map/ppermute | solution.py:15
  32.5 2.0 all-gather
  34.5 0.7 bitcast_add_fusion.18
  35.4 16.8 %all-gather.3 = f32[8,1,2]{2,1,0:T(1,128)S(1)} all-gather(f32[1,1,2]{2,1,0:T(1,128)S(1)} %get-tuple-element.414), channel_id=1, replica_groups=mesh['seq_0'=8,'seq_1'=8,'seq_2'=2,'head'=4] {'seq_1'}, dimensions={0}, use_global_device_ids=true | all-gather | bytes 72 | tf_op jit(solution)/shard_map/all_gather | solution.py:29
  52.1 15.2 %all-gather.4 = f32[8,1,2]{2,1,0:T(1,128)S(1)} all-gather(f32[1,1,2]{2,1,0:T(1,128)S(1)} %get-tuple-element.386), channel_id=1, replica_groups=mesh['seq_0'=8,'seq_1'=8,'seq_2'=2,'head'=4] {'seq_0'}, dimensions={0}, use_global_device_ids=true | all-gather | bytes 72 | tf_op jit(solution)/shard_map/all_gather | solution.py:29
  67.3 15.1 %all-gather.5 = f32[8,1,2]{2,1,0:T(1,128)S(1)} all-gather(f32[1,1,2]{2,1,0:T(1,128)S(1)} %get-tuple-element.385), channel_id=1, replica_groups=mesh['seq_0'=8,'seq_1'=8,'seq_2'=2,'head'=4] {'seq_0'}, dimensions={0}, use_global_device_ids=true | all-gather | bytes 72 | tf_op jit(solution)/shard_map/all_gather | solution.py:29
  82.4 0.7 copy-done.61
  87.6 2.1 multiply_add_fusion.2
  89.8 0.6 slice_bitcast_fusion.29
  90.4 0.6 slice_bitcast_fusion.22
  91.1 0.9 fusion.160
  92.0 1.3 fusion.144
  97.9 0.8 copy-done.17
  99.0 1.4 conditional.13
  99.0 1.4 fusion.10
  100.4 1.8 conditional.14
  100.4 0.8 copy.277
  101.2 1.0 copy.275
  102.3 1.0 multiply_reduce_fusion
  103.3 2.7 %all-gather.11.cloned.1.call-done = f32[8,2,256,64]{2,3,1,0:T(8,128)} async-done(((f32[1,2,256,64]{2,3,1,0:T(8,128)}), f32[8,2,256,64]{2,3,1,0:T(8,128)}) %all-gather.11.cloned.1.call-update) | async-done | bytes 1048592 | tf_op jit(solution)/shard_map/all_gather | solution.py:29
  106.0 0.6 copy-done.23
  106.7 2.1 multiply_add_fusion.3
  108.8 0.7 copy-done.20
  110.4 2.3 %conditional.15 = (f32[256,2,128]{2,0,1:T(8,128)S(1)}, f32[256,2,128]{2,0,1:T(8,128)S(1)}, f32[256,2,128]{2,0,1:T(8,128)S(1)}) conditional(s32[]{:T(128)} %convert_element_type.93, f32[256,2,128]{2,0,1:T(8,128)S(1)} %convolution_bitcast_fusion.8, (pred[256,256]{1,0:T(8,128)(4,1)S(1)}, bf16[256,2,128]{0,2,1:T(8,128)(2,1)S(1)}, ...), branch_computations={%region_20.21_spmd, %region_21.22_spmd} | conditional | flops 169148416 | bytes 4397080 | solution.py:67
  110.8 1.2 fusion.45
  112.8 0.7 copy-done.4
  113.5 0.8 copy.228
  114.4 3.0 %collective-permute-start.5 = (f32[256,2,128]{0,2,1:T(8,128)}, f32[256,2,128]{0,2,1:T(8,128)}, u32[]{:S(2)}, u32[]{:S(2)}) collective-permute-start(f32[256,2,128]{0,2,1:T(8,128)} %copy.228), channel_id=1, source_target_pairs={{8,0},{12,4},{16,8},{20,12},{24,16},{28,20},{32,24},{36,28},{40,32... | collective-permute-start | bytes 786440 | tf_op jit(solution)/shard_map/ppermute | solution.py:15
  117.4 0.8 copy.227
  118.3 2.0 collective-permute-start.4
  120.7 0.9 copy.231
  121.6 2.8 %collective-permute-start.7 = (f32[256,2,128]{0,2,1:T(8,128)}, f32[256,2,128]{0,2,1:T(8,128)}, u32[]{:S(2)}, u32[]{:S(2)}) collective-permute-start(f32[256,2,128]{0,2,1:T(8,128)} %copy.231), channel_id=1, source_target_pairs={{8,0},{12,4},{16,8},{20,12},{24,16},{28,20},{32,24},{36,28},{40,32... | collective-permute-start | bytes 786440 | tf_op jit(solution)/shard_map/ppermute | solution.py:15
  124.4 0.9 copy.230
  125.3 5.6 %collective-permute-start.6 = (f32[256,2,128]{0,2,1:T(8,128)}, f32[256,2,128]{0,2,1:T(8,128)}, u32[]{:S(2)}, u32[]{:S(2)}) collective-permute-start(f32[256,2,128]{0,2,1:T(8,128)} %copy.230), channel_id=1, source_target_pairs={{4,0},{8,4},{12,8},{16,12},{20,16},{24,20},{28,24},{32,28},{36,32}... | collective-permute-start | bytes 786440 | tf_op jit(solution)/shard_map/ppermute | solution.py:15
  130.9 0.7 copy_bitcast_fusion
  131.8 1.3 fusion.68
  133.0 0.8 copy.239
  133.8 14.2 %all-gather.17.cloned.1.call-done = f32[8,2,256,64]{2,3,1,0:T(8,128)} async-done(((f32[1,2,256,64]{2,3,1,0:T(8,128)}), f32[8,2,256,64]{2,3,1,0:T(8,128)}) %all-gather.17.cloned.1.call-update) | async-done | bytes 1048592 | tf_op jit(solution)/shard_map/all_gather | solution.py:29
  148.6 1.7 fusion.98
  151.0 1.1 broadcast_in_dim.229
  152.1 4.4 %all-to-all-start = ((f32[4,256,256]{2,1,0:T(8,128)}), f32[4,256,256]{2,1,0:T(8,128)S(1)}, u32[]{:S(2)}, u32[]{:S(2)}) async-start(f32[4,256,256]{2,1,0:T(8,128)} %broadcast_in_dim.229), calls=%async_computation | async-start | bytes 2097152 | tf_op jit(solution)/shard_map/all_to_all | solution.py:41
  156.5 1.5 fusion.69
  158.0 0.8 copy.240
  158.8 29.7 %all-gather.13.cloned.1.call-done = f32[8,2,256,64]{2,3,1,0:T(8,128)} async-done(((f32[1,2,256,64]{2,3,1,0:T(8,128)}), f32[8,2,256,64]{2,3,1,0:T(8,128)}) %all-gather.13.cloned.1.call-update) | async-done | bytes 1048592 | tf_op jit(solution)/shard_map/all_gather | solution.py:29
  188.5 0.6 copy-done.25
  189.2 1.8 fusion.109
  191.8 1.1 broadcast_in_dim.230
  192.9 4.2 %all-to-all-start.1 = ((f32[4,256,256]{2,1,0:T(8,128)}), f32[4,256,256]{2,1,0:T(8,128)S(1)}, u32[]{:S(2)}, u32[]{:S(2)}) async-start(f32[4,256,256]{2,1,0:T(8,128)} %broadcast_in_dim.230), calls=%async_computation.1 | async-start | bytes 2097152 | tf_op jit(solution)/shard_map/all_to_all | solution.py:41
  197.5 0.6 copy-done.10
  198.6 0.7 copy.241
  200.3 0.7 copy.242
  201.0 0.8 reduce_sum.112
  201.8 6.2 %all-to-all-done.1 = f32[4,256,256]{2,1,0:T(8,128)S(1)} async-done(((f32[4,256,256]{2,1,0:T(8,128)}), f32[4,256,256]{2,1,0:T(8,128)S(1)}, u32[]{:S(2)}, u32[]{:S(2)}) %all-to-all-start.1) | async-done | bytes 1048608 | tf_op jit(solution)/shard_map/all_to_all | solution.py:41
  208.0 0.8 reduce_sum.113
  (221 shorter events, 16.6 us)
Async XLA Ops:
  7.2 5.9 %copy-start = (bf16[256,256]{1,0:T(8,128)(2,1)S(1)}, bf16[256,256]{1,0:T(8,128)(2,1)}, u32[]{:S(2)}) copy-start(bf16[256,256]{1,0:T(8,128)(2,1)} %param.30) | copy-start | bytes 393220
  7.2 80.1 %all-gather.15.cloned.1.call-start = ((), (), s32[]{:S(2)}) async-start(), calls=%async_computation.4 | async-start | bytes 1179648 | tf_op jit(solution)/shard_map/all_gather | solution.py:29
  11.4 4.0 %copy-start.56 = (f32[2]{0:T(128)}, f32[2]{0:T(128)S(1)}, u32[]{:S(2)}) copy-start(f32[2]{0:T(128)S(1)} %get-tuple-element.415) | copy-start | bytes 28
  11.4 23.1 %copy-start.55 = (f32[2]{0:T(128)}, f32[2]{0:T(128)S(1)}, u32[]{:S(2)}) copy-start(f32[2]{0:T(128)S(1)} %get-tuple-element.416) | copy-start | bytes 28
  11.4 3.9 %copy-start.50 = (f32[2]{0:T(128)}, f32[2]{0:T(128)S(1)}, u32[]{:S(2)}) copy-start(f32[2]{0:T(128)S(1)} %get-tuple-element.412) | copy-start | bytes 28
  11.4 23.1 %copy-start.49 = (f32[2]{0:T(128)}, f32[2]{0:T(128)S(1)}, u32[]{:S(2)}) copy-start(f32[2]{0:T(128)S(1)} %get-tuple-element.413) | copy-start | bytes 28
  16.1 0.9 copy-start.8
  16.1 7.5 %copy-start.13 = (bf16[256,256]{1,0:T(8,128)(2,1)S(1)}, bf16[256,256]{1,0:T(8,128)(2,1)}, u32[]{:S(2)}) copy-start(bf16[256,256]{1,0:T(8,128)(2,1)} %param.26) | copy-start | bytes 393220
  16.1 89.8 %all-gather.11.cloned.1.call-start = ((), (), s32[]{:S(2)}) async-start(), calls=%async_computation.2 | async-start | bytes 1179648 | tf_op jit(solution)/shard_map/all_gather | solution.py:29
  17.1 15.0 %copy-start.15 = (bf16[256,128]{1,0:T(8,128)(2,1)S(1)}, bf16[256,128]{1,0:T(8,128)(2,1)}, u32[]{:S(2)}) copy-start(bf16[256,128]{1,0:T(8,128)(2,1)} %param.28) | copy-start | bytes 196612
  17.1 80.1 %collective-permute-start = (bf16[256,256]{0,1:T(8,128)(2,1)S(1)}, bf16[256,256]{0,1:T(8,128)(2,1)S(1)}, u32[]{:S(2)}, u32[]{:S(2)}) collective-permute-start(bf16[256,256]{0,1:T(8,128)(2,1)S(1)} %copy.192), channel_id=1, source_target_pairs={{0,4},{4,8},{8,12},{12,16},{16,20},{20,24},{24,28},{28,32},{32,36}... | collective-permute-start | bytes 393224 | tf_op jit(solution)/shard_map/ppermute | solution.py:15
  19.4 78.4 %collective-permute-start.1 = (bf16[256,256]{0,1:T(8,128)(2,1)S(1)}, bf16[256,256]{0,1:T(8,128)(2,1)S(1)}, u32[]{:S(2)}, u32[]{:S(2)}) collective-permute-start(bf16[256,256]{0,1:T(8,128)(2,1)S(1)} %copy.192), channel_id=1, source_target_pairs={{0,8},{4,12},{8,16},{12,20},{16,24},{20,28},{24,32},{28,36},{32,40... | collective-permute-start | bytes 393224 | tf_op jit(solution)/shard_map/ppermute | solution.py:15
  23.8 8.5 %copy-start.3 = (bf16[256,256]{1,0:T(8,128)(2,1)S(1)}, bf16[256,256]{1,0:T(8,128)(2,1)}, u32[]{:S(2)}) copy-start(bf16[256,256]{1,0:T(8,128)(2,1)} %param.29) | copy-start | bytes 393220
  23.8 75.2 %collective-permute-start.2 = (bf16[256,256]{0,1:T(8,128)(2,1)S(1)}, bf16[256,256]{0,1:T(8,128)(2,1)}, u32[]{:S(2)}, u32[]{:S(2)}) collective-permute-start(bf16[256,256]{0,1:T(8,128)(2,1)S(1)} %copy.202), channel_id=1, source_target_pairs={{0,4},{4,8},{8,12},{12,16},{16,20},{20,24},{24,28},{28,32},{32,36}... | collective-permute-start | bytes 393224 | tf_op jit(solution)/shard_map/ppermute | solution.py:15
  27.8 72.6 %collective-permute-start.3 = (bf16[256,256]{0,1:T(8,128)(2,1)S(1)}, bf16[256,256]{0,1:T(8,128)(2,1)}, u32[]{:S(2)}, u32[]{:S(2)}) collective-permute-start(bf16[256,256]{0,1:T(8,128)(2,1)S(1)} %copy.202), channel_id=1, source_target_pairs={{0,8},{4,12},{8,16},{12,20},{16,24},{20,28},{24,32},{28,36},{32,40... | collective-permute-start | bytes 393224 | tf_op jit(solution)/shard_map/ppermute | solution.py:15
  35.3 112.7 %all-gather.17.cloned.1.call-start = ((), (), s32[]{:S(2)}) async-start(), calls=%async_computation.5 | async-start | bytes 1179648 | tf_op jit(solution)/shard_map/all_gather | solution.py:29
  83.0 0.9 copy-start.11
  84.8 2.4 %copy-start.16 = (pred[256,256]{0,1:T(8,128)(4,1)}, pred[256,256]{0,1:T(8,128)(4,1)S(1)}, u32[]{:S(2)}) copy-start(pred[256,256]{0,1:T(8,128)(4,1)S(1)} %copy.188) | copy-start | bytes 196612
  85.3 2.0 copy-start.59
  87.3 21.5 %copy-start.9 = (f32[2,256,256]{1,2,0:T(8,128)}, f32[2,256,256]{1,2,0:T(8,128)S(1)}, u32[]{:S(2)}) copy-start(f32[2,256,256]{1,2,0:T(8,128)S(1)} %get-tuple-element.418) | copy-start | bytes 1572868
  89.7 98.8 %all-gather.13.cloned.1.call-start = ((), (), s32[]{:S(2)}) async-start(), calls=%async_computation.3 | async-start | bytes 1179648 | tf_op jit(solution)/shard_map/all_gather | solution.py:29
  91.0 6.0 %copy-start.12 = (bf16[256,256]{1,0:T(8,128)(2,1)S(1)}, bf16[256,256]{1,0:T(8,128)(2,1)}, u32[]{:S(2)}) copy-start(bf16[256,256]{1,0:T(8,128)(2,1)} %param.27) | copy-start | bytes 393220
  97.9 2.6 %copy-start.19 = (f32[2,256]{1,0:T(2,128)}, f32[2,256]{1,0:T(2,128)S(1)}, u32[]{:S(2)}) copy-start(f32[2,256]{1,0:T(2,128)S(1)} %get-tuple-element.171) | copy-start | bytes 6148
  102.2 1.0 copy-start.14
  102.2 3.8 %copy-start.35 = (f32[2]{0:T(128)S(1)}, f32[2]{0:T(128)}, u32[]{:S(2)}) copy-start(f32[2]{0:T(128)} %copy-done.34) | copy-start | bytes 28
  102.2 3.8 %copy-start.38 = (f32[2]{0:T(128)S(1)}, f32[2]{0:T(128)}, u32[]{:S(2)}) copy-start(f32[2]{0:T(128)} %copy-done.37) | copy-start | bytes 28
  102.2 3.8 %copy-start.41 = (f32[2]{0:T(128)S(1)}, f32[2]{0:T(128)}, u32[]{:S(2)}) copy-start(f32[2]{0:T(128)} %copy-done.40) | copy-start | bytes 28
  102.2 3.8 %copy-start.52 = (f32[2]{0:T(128)S(1)}, f32[2]{0:T(128)}, u32[]{:S(2)}) copy-start(f32[2]{0:T(128)} %get-tuple-element.388) | copy-start | bytes 28
  102.3 3.8 %copy-start.58 = (f32[2]{0:T(128)S(1)}, f32[2]{0:T(128)}, u32[]{:S(2)}) copy-start(f32[2]{0:T(128)} %get-tuple-element.396) | copy-start | bytes 28
  114.4 17.2 %collective-permute-start.5 = (f32[256,2,128]{0,2,1:T(8,128)}, f32[256,2,128]{0,2,1:T(8,128)}, u32[]{:S(2)}, u32[]{:S(2)}) collective-permute-start(f32[256,2,128]{0,2,1:T(8,128)} %copy.228), channel_id=1, source_target_pairs={{8,0},{12,4},{16,8},{20,12},{24,16},{28,20},{32,24},{36,28},{40,32... | collective-permute-start | bytes 786440 | tf_op jit(solution)/shard_map/ppermute | solution.py:15
  117.4 2.9 %copy-start.47 = (f32[1,2,2,128]{3,1,2,0:T(2,128)S(1)}, f32[1,2,2,128]{3,1,2,0:T(2,128)}, u32[]{:S(2)}) copy-start(f32[1,2,2,128]{3,1,2,0:T(2,128)} %copy-done.46) | copy-start | bytes 6148
  118.2 2.1 copy-start.44
  118.3 13.3 %collective-permute-start.4 = (f32[256,2,128]{0,2,1:T(8,128)}, f32[256,2,128]{0,2,1:T(8,128)}, u32[]{:S(2)}, u32[]{:S(2)}) collective-permute-start(f32[256,2,128]{0,2,1:T(8,128)} %copy.227), channel_id=1, source_target_pairs={{4,0},{8,4},{12,8},{16,12},{20,16},{24,20},{28,24},{32,28},{36,32}... | collective-permute-start | bytes 786440 | tf_op jit(solution)/shard_map/ppermute | solution.py:15
  120.7 3.7 %copy-start.5 = (f32[256,2,128]{2,0,1:T(8,128)S(1)}, f32[256,2,128]{2,0,1:T(8,128)}, u32[]{:S(2)}) copy-start(f32[256,2,128]{2,0,1:T(8,128)} %copy-done.4) | copy-start | bytes 786436
  121.6 34.9 %collective-permute-start.7 = (f32[256,2,128]{0,2,1:T(8,128)}, f32[256,2,128]{0,2,1:T(8,128)}, u32[]{:S(2)}, u32[]{:S(2)}) collective-permute-start(f32[256,2,128]{0,2,1:T(8,128)} %copy.231), channel_id=1, source_target_pairs={{8,0},{12,4},{16,8},{20,12},{24,16},{28,20},{32,24},{36,28},{40,32... | collective-permute-start | bytes 786440 | tf_op jit(solution)/shard_map/ppermute | solution.py:15
  124.4 7.2 %copy-start.7 = (bf16[2,256,256]{1,2,0:T(8,128)(2,1)S(1)}, bf16[2,256,256]{1,2,0:T(8,128)(2,1)}, u32[]{:S(2)}) copy-start(bf16[2,256,256]{1,2,0:T(8,128)(2,1)} %copy-done.6) | copy-start | bytes 786436
  124.4 23.6 %copy-start.2 = (f32[8,2,256,64]{2,3,1,0:T(8,128)S(1)}, f32[8,2,256,64]{2,3,1,0:T(8,128)}, u32[]{:S(2)}) copy-start(f32[8,2,256,64]{2,3,1,0:T(8,128)} %all-gather.15.cloned.1.call-done) | copy-start | bytes 3145732
  125.3 31.2 %collective-permute-start.6 = (f32[256,2,128]{0,2,1:T(8,128)}, f32[256,2,128]{0,2,1:T(8,128)}, u32[]{:S(2)}, u32[]{:S(2)}) collective-permute-start(f32[256,2,128]{0,2,1:T(8,128)} %copy.230), channel_id=1, source_target_pairs={{4,0},{8,4},{12,8},{16,12},{20,16},{24,20},{28,24},{32,28},{36,32}... | collective-permute-start | bytes 786440 | tf_op jit(solution)/shard_map/ppermute | solution.py:15
  131.6 16.4 %copy-start.36 = (f32[2]{0:T(128)S(1)}, f32[2]{0:T(128)}, u32[]{:S(2)}) copy-start(f32[2]{0:T(128)} %copy-done.34) | copy-start | bytes 28
  131.6 16.4 %copy-start.39 = (f32[2]{0:T(128)S(1)}, f32[2]{0:T(128)}, u32[]{:S(2)}) copy-start(f32[2]{0:T(128)} %copy-done.37) | copy-start | bytes 28
  131.6 16.4 %copy-start.42 = (f32[2]{0:T(128)S(1)}, f32[2]{0:T(128)}, u32[]{:S(2)}) copy-start(f32[2]{0:T(128)} %copy-done.40) | copy-start | bytes 28
  131.6 16.4 %copy-start.51 = (f32[2]{0:T(128)S(1)}, f32[2]{0:T(128)}, u32[]{:S(2)}) copy-start(f32[2]{0:T(128)} %copy-done.50) | copy-start | bytes 28
  131.6 16.4 %copy-start.54 = (f32[2]{0:T(128)S(1)}, f32[2]{0:T(128)}, u32[]{:S(2)}) copy-start(f32[2]{0:T(128)} %copy-done.53) | copy-start | bytes 28
  131.6 16.4 %copy-start.57 = (f32[2]{0:T(128)S(1)}, f32[2]{0:T(128)}, u32[]{:S(2)}) copy-start(f32[2]{0:T(128)} %copy-done.56) | copy-start | bytes 28
  131.7 16.4 %copy-start.60 = (f32[2]{0:T(128)S(1)}, f32[2]{0:T(128)}, u32[]{:S(2)}) copy-start(f32[2]{0:T(128)} %copy-done.59) | copy-start | bytes 28
  131.7 16.4 %copy-start.62 = (f32[2]{0:T(128)S(1)}, f32[2]{0:T(128)}, u32[]{:S(2)}) copy-start(f32[2]{0:T(128)} %get-tuple-element.369) | copy-start | bytes 28
  131.7 16.4 %copy-start.63 = (f32[2]{0:T(128)S(1)}, f32[2]{0:T(128)}, u32[]{:S(2)}) copy-start(f32[2]{0:T(128)} %get-tuple-element.370) | copy-start | bytes 28
  131.7 16.4 %copy-start.64 = (f32[2]{0:T(128)S(1)}, f32[2]{0:T(128)}, u32[]{:S(2)}) copy-start(f32[2]{0:T(128)} %get-tuple-element.377) | copy-start | bytes 28
  131.7 16.4 %copy-start.65 = (f32[2]{0:T(128)S(1)}, f32[2]{0:T(128)}, u32[]{:S(2)}) copy-start(f32[2]{0:T(128)} %get-tuple-element.378) | copy-start | bytes 28
  131.7 16.4 %copy-start.66 = (f32[2]{0:T(128)S(1)}, f32[2]{0:T(128)}, u32[]{:S(2)}) copy-start(f32[2]{0:T(128)} %get-tuple-element.379) | copy-start | bytes 28
  131.7 16.4 %copy-start.67 = (f32[2]{0:T(128)S(1)}, f32[2]{0:T(128)}, u32[]{:S(2)}) copy-start(f32[2]{0:T(128)} %get-tuple-element.380) | copy-start | bytes 28
  131.7 16.4 %copy-start.68 = (f32[2]{0:T(128)S(1)}, f32[2]{0:T(128)}, u32[]{:S(2)}) copy-start(f32[2]{0:T(128)} %get-tuple-element.381) | copy-start | bytes 28
  131.7 16.4 %copy-start.69 = (f32[2]{0:T(128)S(1)}, f32[2]{0:T(128)}, u32[]{:S(2)}) copy-start(f32[2]{0:T(128)} %get-tuple-element.382) | copy-start | bytes 28
  131.7 16.4 %copy-start.70 = (f32[2]{0:T(128)S(1)}, f32[2]{0:T(128)}, u32[]{:S(2)}) copy-start(f32[2]{0:T(128)} %get-tuple-element.383) | copy-start | bytes 28
  131.8 16.4 %copy-start.71 = (f32[2]{0:T(128)S(1)}, f32[2]{0:T(128)}, u32[]{:S(2)}) copy-start(f32[2]{0:T(128)} %get-tuple-element.384) | copy-start | bytes 28
  152.1 4.4 %copy-start.18 = (pred[256,256]{0,1:T(8,128)(4,1)S(1)}, pred[256,256]{0,1:T(8,128)(4,1)}, u32[]{:S(2)}) copy-start(pred[256,256]{0,1:T(8,128)(4,1)} %copy-done.16) | copy-start | bytes 196612
  152.1 4.4 %copy-start.21 = (f32[2,256]{1,0:T(2,128)S(1)}, f32[2,256]{1,0:T(2,128)}, u32[]{:S(2)}) copy-start(f32[2,256]{1,0:T(2,128)} %copy-done.19) | copy-start | bytes 6148
  152.1 39.7 %all-to-all-start = ((f32[4,256,256]{2,1,0:T(8,128)}), f32[4,256,256]{2,1,0:T(8,128)S(1)}, u32[]{:S(2)}, u32[]{:S(2)}) async-start(f32[4,256,256]{2,1,0:T(8,128)} %broadcast_in_dim.229), calls=%async_computation | async-start | bytes 2097152 | tf_op jit(solution)/shard_map/all_to_all | solution.py:41
  156.5 32.1 %copy-start.1 = (f32[8,2,256,64]{2,3,1,0:T(8,128)S(1)}, f32[8,2,256,64]{2,3,1,0:T(8,128)}, u32[]{:S(2)}) copy-start(f32[8,2,256,64]{2,3,1,0:T(8,128)} %all-gather.11.cloned.1.call-done) | copy-start | bytes 3145732
  192.9 15.1 %all-to-all-start.1 = ((f32[4,256,256]{2,1,0:T(8,128)}), f32[4,256,256]{2,1,0:T(8,128)S(1)}, u32[]{:S(2)}, u32[]{:S(2)}) async-start(f32[4,256,256]{2,1,0:T(8,128)} %broadcast_in_dim.230), calls=%async_computation.1 | async-start | bytes 2097152 | tf_op jit(solution)/shard_map/all_to_all | solution.py:41
  197.1 0.9 copy-start.10
  197.1 1.0 copy-start.45
  197.1 1.0 copy-start.48
  197.1 0.9 copy-start.72
  (23 other events, 14.9 us)
Sparse Core Ops, SparseCore 0:
  16.2 46.4 all-gather.14
  65.4 40.5 all-gather.10
  108.1 39.8 all-gather.16
  149.9 38.5 all-gather.12
where the time goes:
time: 216 us; the launch traced here: 215 us
  waiting for transfers between devices  53 us (25%)
  blocking collectives  52.8 us (24%)
  starting transfers between devices  37.1 us (17%)
  local copies, waits for them, and re-layouts  22.9 us (11%)
  other arithmetic  19.2 us (9%)
  between operations  17.5 us (8%)
  matrix products  12.8 us (6%)
    all_gather x6, blocking collectives, carried_in(): pieces = jax.tree.map(lambda part: lax.all_gather(part, axis), subtotal)  52.8 us
    all_gather x4, waiting for transfers between devices, carried_in(): pieces = jax.tree.map(lambda part: lax.all_gather(part, axis), subtotal)  46.6 us
    ppermute x8, starting transfers between devices, shifted(): return lax.ppermute(x, axis, pairs)  28.3 us
    unnamed x157, local copies, waits for them, and re-layouts  12.5 us
    all_to_all x2, starting transfers between devices, from_everyone(): return lax.all_to_all(copies, axis, split_axis=0, concat_axis=0, tiled=True)  8.6 us
    add x5, other arithmetic, chained(): later_item[0][:, None, None] * earlier[1] + later_item[1]  7.37 us
    all_to_all x2, waiting for transfers between devices, from_everyone(): return lax.all_to_all(copies, axis, split_axis=0, concat_axis=0, tiled=True)  6.24 us
  transfers between devices with their start and end apart: 14, of which 4 were waited for; matrix products, arithmetic and copies ran while one was open for 19% of the time, Pallas kernels for 0%

commit v1 on v0

v1 whole, which is shorter than its diff:
```python
import functools

import jax
import jax.numpy as jnp
from jax import lax
from jax.experimental import pallas as pl
from jax.experimental.pallas import tpu as pltpu
from jax.sharding import PartitionSpec as P

MESH = pl.DeviceIdType.MESH
HEAD_DIM = 128
SCALE = HEAD_DIM**-0.5
OFF = -1e30
F32 = jnp.float32
BF16 = jnp.bfloat16
VMEM_BYTES = 40 * 1024 * 1024


def dot(a, b):
    return jnp.dot(a, b, preferred_element_type=F32)


def dot_nt(a, b):
    return lax.dot_general(a, b, (((1,), (1,)), ((), ())), preferred_element_type=F32)


def dot_tn(a, b):
    return lax.dot_general(a, b, (((0,), (0,)), ((), ())), preferred_element_type=F32)


def iota(shape, axis):
    return lax.broadcasted_iota(jnp.int32, shape, axis)


def lower(size):
    return iota((size, size), 1) <= iota((size, size), 0)


def doc_start_column(doc_ref, first, rows):
    docs = doc_ref.shape[1]
    lengths = jnp.broadcast_to(doc_ref[...], (16, docs))
    upper = jnp.where(iota((docs, docs), 0) <= iota((docs, docs), 1), 1.0, 0.0).astype(BF16)
    high, low = lengths // 16, lengths % 16
    ends = 16.0 * dot(high.astype(F32).astype(BF16), upper) + dot(
        low.astype(F32).astype(BF16), upper
    )
    ends = jnp.broadcast_to(ends[0:1, :], (rows, docs))
    position = (first + iota((rows, docs), 0)).astype(F32)
    return jnp.max(jnp.where(ends <= position, ends, 0.0), axis=1, keepdims=True)


def running_sum(rows):
    ones = jnp.where(lower(rows.shape[0]), 1.0, 0.0).astype(BF16)
    high = rows.astype(BF16)
    rest = rows - high.astype(F32)
    middle = rest.astype(BF16)
    low = (rest - middle.astype(F32)).astype(BF16)
    return dot(ones, high) + dot(ones, middle) + dot(ones, low)


def main_kernel(
    n_seq,
    n_head,
    n_z,
    rate_ref,
    gain_ref,
    doc_ref,
    q_ref,
    k_ref,
    v_ref,
    do_ref,
    x_ref,
    g_ref,
    b_ref,
    c_ref,
    dt_ref,
    attn_ref,
    dq_ref,
    dk_ref,
    dv_ref,
    y_ref,
    xg_ref,
    mix_ref,
    state_ref,
    kv_in,
    qd_in,
    stat_out,
    stat_in,
    a_src,
    a_dst,
    la_src,
    la_dst,
    scan_buf,
    cum_buf,
    t_src,
    t_dst,
    tl_src,
    tl_dst,
    r_src,
    r_dst,
    near_send,
    near_recv,
    stat_send,
    stat_recv,
    a_send,
    a_recv,
    la_send,
    la_recv,
    t_send,
    t_recv,
    tl_send,
    tl_recv,
    r_send,
    r_recv,
    mix_send,
    mix_recv,
    state_send,
    state_recv,
):
    me = lax.axis_index("seq")
    hx = lax.axis_index("head")
    row = 2 * n_z
    n_y = n_seq // row
    rows = q_ref.shape[0]
    group, pos = me // row, me % row
    core = pos % 2
    base = group * row
    width = rows // n_z

    def seq_at(offset):
        return (me + offset + n_seq) % n_seq

    def slot_of(index, count, side):
        return index + side * (count - 1 - 2 * index)

    barrier = pltpu.get_barrier_semaphore()

    def greet(seq_index, head_index):
        pl.semaphore_signal(
            barrier, inc=1, device_id=(seq_index, head_index), device_id_type=MESH
        )

    for offset in (-2, -1, 1, 2):
        greet(seq_at(offset), hx)

    def greet_row(k, carry):
        greet(base + (pos + k) % row, hx)
        return carry

    lax.fori_loop(1, row, greet_row, 0)

    def greet_group(k, carry):
        greet(((group + k) % n_y) * row + pos, hx)
        return carry

    lax.fori_loop(1, n_y, greet_group, 0)
    for k in range(1, n_head):
        greet(me, (hx + k) % n_head)

    lanes_low = iota((rows, 128), 1) < 64
    dt_wide = jnp.concatenate(
        [
            jnp.broadcast_to(dt_ref[0:1, :], (64, rows)),
            jnp.broadcast_to(dt_ref[1:2, :], (64, rows)),
        ],
        axis=0,
    ).T
    rate_wide = jnp.where(lanes_low, rate_ref[0], rate_ref[1])
    gain_wide = jnp.where(lanes_low, gain_ref[0], gain_ref[1])
    log_decay = running_sum(-dt_wide * rate_wide)
    carry_weight = jnp.exp(log_decay)
    source_weight = jnp.exp(-log_decay) * dt_wide
    last = log_decay[rows - 1 : rows, :]
    decay_all = jnp.exp(last)
    mix_ref[hx, 0] = (carry_weight * g_ref[...].astype(F32)).astype(BF16)
    mix_ref[hx, 1] = (source_weight * x_ref[...].astype(F32)).astype(BF16)
    local_state = (decay_all * dot_tn(b_ref[...], mix_ref[hx, 1])).astype(BF16)
    local_adjoint = dot_tn(c_ref[...], mix_ref[hx, 0]).astype(BF16)
    for z in range(n_z):
        a_src[2 * z] = local_state[z * width : (z + 1) * width, :]
        a_src[2 * z + 1] = local_adjoint[z * width : (z + 1) * width, :]
    la_src[...] = last

    pl.semaphore_wait(barrier, 4 + (row - 1) + (n_y - 1) + (n_head - 1))

    def a_copies(k):
        owner = (pos + k) % row
        slot = slot_of(pos, row, owner % 2)
        target = (base + owner, hx)
        return (
            pltpu.make_async_remote_copy(
                a_src.at[owner], a_dst.at[slot], a_send.at[k], a_recv.at[slot], target, MESH
            ),
            pltpu.make_async_remote_copy(
                la_src, la_dst.at[slot], la_send.at[k], la_recv.at[slot], target, MESH
            ),
        )

    def a_start(k, carry):
        for copy in a_copies(k):
            copy.start()
        return carry

    lax.fori_loop(1, row, a_start, 0)
    own_slot = slot_of(pos, row, core)
    a_dst[own_slot] = a_src[pos]
    la_dst[own_slot] = la_src[...]

    near = []
    for distance in (1, 2):
        for part, (fore, back) in enumerate(((k_ref, q_ref), (v_ref, do_ref))):
            at = (distance - 1) * 2 + part
            near.append(
                pltpu.make_async_remote_copy(
                    fore,
                    kv_in.at[distance - 1, part],
                    near_send.at[at],
                    near_recv.at[at],
                    (seq_at(distance), hx),
                    MESH,
                )
            )
            near.append(
                pltpu.make_async_remote_copy(
                    back,
                    qd_in.at[distance - 1, part],
                    near_send.at[4 + at],
                    near_recv.at[4 + at],
                    (seq_at(-distance), hx),
                    MESH,
                )
            )
    for copy in near:
        copy.start()

    def over_head(ref, send, recv):
        return [
            pltpu.make_async_remote_copy(
                ref.at[hx],
                ref.at[hx],
                send.at[k],
                recv.at[hx],
                (me, (hx + k) % n_head),
                MESH,
            )
            for k in range(1, n_head)
        ]

    def from_head(ref, send, recv):
        for k in range(1, n_head):
            other = (hx + k) % n_head
            pltpu.make_async_remote_copy(
                ref.at[hx], ref.at[other], send.at[k], recv.at[other], (me, other), MESH
            ).wait_recv()

    mix_copies = over_head(mix_ref, mix_send, mix_recv)
    for copy in mix_copies:
        copy.start()

    causal = lower(rows)
    meet = jnp.where(causal, dot_nt(c_ref[...], b_ref[...]), 0.0).astype(BF16)
    y_inner = dot(meet, mix_ref[hx, 1])
    meet_back = jnp.where(
        iota((rows, rows), 0) <= iota((rows, rows), 1), dot_nt(b_ref[...], c_ref[...]), 0.0
    ).astype(BF16)
    x_inner = dot(meet_back, mix_ref[hx, 0])

    def a_wait(k, carry):
        slot = (own_slot + k) % row
        pltpu.make_async_remote_copy(
            a_src.at[0], a_dst.at[slot], a_send.at[k], a_recv.at[slot], (me, hx), MESH
        ).wait_recv()
        pltpu.make_async_remote_copy(
            la_src, la_dst.at[slot], la_send.at[k], la_recv.at[slot], (me, hx), MESH
        ).wait_recv()
        return carry

    lax.fori_loop(1, row, a_wait, 0)

    state = jnp.zeros((width, 128), F32)
    summed = jnp.zeros((1, 128), F32)
    for slot in range(row):
        scan_buf[slot] = state
        cum_buf[slot] = summed
        state = jnp.exp(la_dst[slot]) * state + a_dst[slot].astype(F32)
        summed = summed + la_dst[slot]
    t_src[...] = state.astype(BF16)
    tl_src[...] = summed

    own_group = slot_of(group, n_y, core)

    def t_copies(k):
        target = (((group + k) % n_y) * row + pos, hx)
        return (
            pltpu.make_async_remote_copy(
                t_src, t_dst.at[own_group], t_send.at[k], t_recv.at[own_group], target, MESH
            ),
            pltpu.make_async_remote_copy(
                tl_src, tl_dst.at[own_group], tl_send.at[k], tl_recv.at[own_group], target, MESH
            ),
        )

    def t_start(k, carry):
        for copy in t_copies(k):
            copy.start()
        return carry

    lax.fori_loop(1, n_y, t_start, 0)
    t_dst[own_group] = t_src[...]
    tl_dst[own_group] = tl_src[...]

    first = me * rows
    start_column = doc_start_column(doc_ref, first, rows)

    def t_wait(k, carry):
        slot = (own_group + k) % n_y
        pltpu.make_async_remote_copy(
            t_src, t_dst.at[slot], t_send.at[k], t_recv.at[slot], (me, hx), MESH
        ).wait_recv()
        pltpu.make_async_remote_copy(
            tl_src, tl_dst.at[slot], tl_send.at[k], tl_recv.at[slot], (me, hx), MESH
        ).wait_recv()
        return carry

    lax.fori_loop(1, n_y, t_wait, 0)
    carried = jnp.zeros((width, 128), F32)
    for slot in range(n_y):
        grown = jnp.exp(tl_dst[slot]) * carried + t_dst[slot].astype(F32)
        carried = jnp.where(slot < own_group, grown, carried)
    for slot in range(row):
        r_src[slot] = (scan_buf[slot] + jnp.exp(cum_buf[slot]) * carried).astype(BF16)

    def r_copy(k):
        other = (pos + k) % row
        return pltpu.make_async_remote_copy(
            r_src.at[slot_of(other, row, core)],
            r_dst.at[pos],
            r_send.at[k],
            r_recv.at[pos],
            (base + other, hx),
            MESH,
        )

    def r_start(k, carry):
        r_copy(k).start()
        return carry

    lax.fori_loop(1, row, r_start, 0)
    r_dst[pos] = r_src[own_slot]

    for copy in near:
        copy.wait_recv()
    columns = rows
    query_pos = (first + iota((rows, columns), 0)).astype(F32)
    start_wide = jnp.broadcast_to(start_column, (rows, columns))
    masks = []
    for distance in range(3):
        key_pos = (first - distance * rows + iota((rows, columns), 1)).astype(F32)
        masks.append((key_pos >= start_wide) & (key_pos <= query_pos))
    lane = iota((rows, 128), 1)
    stats = jnp.where(lane == 4, start_column, 0.0)
    for h in range(2):
        cols = slice(h * HEAD_DIM, (h + 1) * HEAD_DIM)
        query, grad = q_ref[:, cols], do_ref[:, cols]
        keys = [k_ref[:, cols], kv_in[0, 0, :, cols], kv_in[1, 0, :, cols]]
        values = [v_ref[:, cols], kv_in[0, 1, :, cols], kv_in[1, 1, :, cols]]
        scores = [
            jnp.where(mask, dot_nt(query, key) * SCALE, OFF) for mask, key in zip(masks, keys)
        ]
        top = jnp.max(
            jnp.maximum(jnp.maximum(scores[0], scores[1]), scores[2]), axis=1, keepdims=True
        )
        powers = [jnp.exp(score - top) for score in scores]
        total = jnp.sum(powers[0] + powers[1] + powers[2], axis=1, keepdims=True)
        inverse = 1.0 / total
        probs = [power * inverse for power in powers]
        out = sum(dot(prob.astype(BF16), value) for prob, value in zip(probs, values))
        out = out.astype(BF16)
        attn_ref[:, cols] = out
        delta = jnp.sum(grad.astype(F32) * out.astype(F32), axis=1, keepdims=True)
        slopes = [
            (prob * (dot_nt(grad, value) - delta) * SCALE).astype(BF16)
            for prob, value in zip(probs, values)
        ]
        dq_ref[:, cols] = sum(dot(slope, key) for slope, key in zip(slopes, keys)).astype(BF16)
        stats = jnp.where(lane == h, top + jnp.log(total), stats)
        stats = jnp.where(lane == 2 + h, delta, stats)
    stat_out[...] = stats.T[0:8, :]
    stat_copies = [
        pltpu.make_async_remote_copy(
            stat_out,
            stat_in.at[distance - 1],
            stat_send.at[distance - 1],
            stat_recv.at[distance - 1],
            (seq_at(-distance), hx),
            MESH,
        )
        for distance in (1, 2)
    ]
    for copy in stat_copies:
        copy.start()

    def r_wait(k, carry):
        other = (pos + k) % row
        pltpu.make_async_remote_copy(
            r_src.at[0], r_dst.at[other], r_send.at[k], r_recv.at[other], (me, hx), MESH
        ).wait_recv()
        return carry

    lax.fori_loop(1, row, r_wait, 0)
    for z in range(n_z):
        part = slice(z * width, (z + 1) * width)
        state_ref[hx, 0, part, :] = r_dst[2 * z]
        state_ref[hx, 1, part, :] = (decay_all * r_dst[2 * z + 1].astype(F32)).astype(BF16)
    state_copies = over_head(state_ref, state_send, state_recv)
    for copy in state_copies:
        copy.start()
    y_ref[...] = (
        carry_weight * (y_inner + dot(c_ref[...], state_ref[hx, 0]))
        + gain_wide * x_ref[...].astype(F32)
    ).astype(BF16)
    xg_ref[...] = (
        source_weight * (x_inner + dot(b_ref[...], state_ref[hx, 1]))
        + gain_wide * g_ref[...].astype(F32)
    ).astype(BF16)

    for copy in stat_copies:
        copy.wait_recv()
    key_pos = (first + iota((rows, columns), 0)).astype(F32)
    turned = []
    for distance in range(3):
        stat = stat_out if distance == 0 else stat_in.at[distance - 1]
        query_pos = (seq_at(distance) * rows + iota((rows, columns), 1)).astype(F32)
        turned.append((key_pos >= stat[4:5, :]) & (key_pos <= query_pos))
    for h in range(2):
        cols = slice(h * HEAD_DIM, (h + 1) * HEAD_DIM)
        key, value = k_ref[:, cols], v_ref[:, cols]
        key_total = value_total = jnp.zeros((rows, HEAD_DIM), F32)
        for distance in range(3):
            if distance == 0:
                stat, query, grad = stat_out, q_ref[:, cols], do_ref[:, cols]
            else:
                stat = stat_in.at[distance - 1]
                query, grad = qd_in[distance - 1, 0, :, cols], qd_in[distance - 1, 1, :, cols]
            score = jnp.where(turned[distance], dot_nt(key, query) * SCALE, OFF)
            prob = jnp.exp(score - stat[h : h + 1, :])
            value_total = value_total + dot(prob.astype(BF16), grad)
            slope = prob * (dot_nt(value, grad) - stat[2 + h : 3 + h, :]) * SCALE
            key_total = key_total + dot(slope.astype(BF16), query)
        dk_ref[:, cols] = key_total.astype(BF16)
        dv_ref[:, cols] = value_total.astype(BF16)

    from_head(mix_ref, mix_send, mix_recv)
    from_head(state_ref, state_send, state_recv)

    for copy in near + mix_copies + state_copies + stat_copies:
        copy.wait_send()

    def row_sent(k, carry):
        for copy in (*a_copies(k), r_copy(k)):
            copy.wait_send()
        return carry

    lax.fori_loop(1, row, row_sent, 0)

    def group_sent(k, carry):
        for copy in t_copies(k):
            copy.wait_send()
        return carry

    lax.fori_loop(1, n_y, group_sent, 0)


def last_kernel(
    n_head,
    b_ref,
    c_ref,
    mix_ref,
    state_ref,
    attn_in,
    dq_in,
    dk_in,
    dv_in,
    y_in,
    xg_in,
    attn_ref,
    dq_ref,
    dk_ref,
    dv_ref,
    y_ref,
    xg_ref,
    bg_ref,
    cg_ref,
):
    rows = b_ref.shape[0]
    causal = lower(rows)
    anti = iota((rows, rows), 0) <= iota((rows, rows), 1)
    meet = sum(dot_nt(mix_ref[h, 0], mix_ref[h, 1]) for h in range(n_head))
    meet = jnp.where(causal, meet, 0.0).astype(BF16)
    cg_ref[...] = dot(meet, b_ref[...]) + sum(
        dot_nt(mix_ref[h, 0], state_ref[h, 0]) for h in range(n_head)
    )
    meet = sum(dot_nt(mix_ref[h, 1], mix_ref[h, 0]) for h in range(n_head))
    meet = jnp.where(anti, meet, 0.0).astype(BF16)
    bg_ref[...] = dot(meet, c_ref[...]) + sum(
        dot_nt(mix_ref[h, 1], state_ref[h, 1]) for h in range(n_head)
    )
    for source, target in (
        (attn_in, attn_ref),
        (dq_in, dq_ref),
        (dk_in, dk_ref),
        (dv_in, dv_ref),
        (y_in, y_ref),
        (xg_in, xg_ref),
    ):
        target[...] = source[...]


def on_device(
    n_seq,
    n_head,
    n_z,
    queries,
    key_rows,
    value_rows,
    attn_out_grad,
    ssm_input,
    b_matrix,
    c_matrix,
    step_sizes,
    decay_rates,
    skip_gain,
    ssm_out_grad,
    doc_lengths,
):
    rows, columns = queries.shape
    row, n_y, width = 2 * n_z, n_seq // (2 * n_z), rows // n_z
    vmem = pl.BlockSpec(memory_space=pltpu.VMEM)
    smem = pl.BlockSpec(memory_space=pltpu.SMEM)
    wide = jax.ShapeDtypeStruct((rows, columns), BF16)
    narrow = jax.ShapeDtypeStruct((rows, 128), BF16)
    stacked = jax.ShapeDtypeStruct((n_head, 2, rows, 128), BF16)
    dma = pltpu.SemaphoreType.DMA
    attn, dq, dk, dv, y, xg, mix, state = pl.pallas_call(
        functools.partial(main_kernel, n_seq, n_head, n_z),
        out_shape=(wide, wide, wide, wide, narrow, narrow, stacked, stacked),
        in_specs=[smem, smem] + [vmem] * 10,
        out_specs=(vmem,) * 8,
        scratch_shapes=[
            pltpu.VMEM((2, 2, rows, columns), BF16),
            pltpu.VMEM((2, 2, rows, columns), BF16),
            pltpu.VMEM((8, rows), F32),
            pltpu.VMEM((2, 8, rows), F32),
            pltpu.VMEM((row, width, 128), BF16),
            pltpu.VMEM((row, width, 128), BF16),
            pltpu.VMEM((1, 128), F32),
            pltpu.VMEM((row, 1, 128), F32),
            pltpu.VMEM((row, width, 128), F32),
            pltpu.VMEM((row, 1, 128), F32),
            pltpu.VMEM((width, 128), BF16),
            pltpu.VMEM((n_y, width, 128), BF16),
            pltpu.VMEM((1, 128), F32),
            pltpu.VMEM((n_y, 1, 128), F32),
            pltpu.VMEM((row, width, 128), BF16),
            pltpu.VMEM((row, width, 128), BF16),
            dma((8,)),
            dma((8,)),
            dma((2,)),
            dma((2,)),
            dma((row,)),
            dma((row,)),
            dma((row,)),
            dma((row,)),
            dma((n_y,)),
            dma((n_y,)),
            dma((n_y,)),
            dma((n_y,)),
            dma((row,)),
            dma((row,)),
            dma((n_head,)),
            dma((n_head,)),
            dma((n_head,)),
            dma((n_head,)),
        ],
        compiler_params=pltpu.CompilerParams(
            collective_id=0, has_side_effects=True, vmem_limit_bytes=VMEM_BYTES
        ),
        name="main",
    )(
        decay_rates,
        skip_gain,
        doc_lengths.reshape(1, -1),
        queries,
        key_rows,
        value_rows,
        attn_out_grad,
        ssm_input,
        ssm_out_grad,
        b_matrix,
        c_matrix,
        step_sizes.T,
    )
    grads = jax.ShapeDtypeStruct((rows, b_matrix.shape[1]), F32)
    return pl.pallas_call(
        functools.partial(last_kernel, n_head),
        out_shape=(wide, wide, wide, wide, narrow, narrow, grads, grads),
        in_specs=[vmem] * 10,
        out_specs=(vmem,) * 8,
        compiler_params=pltpu.CompilerParams(vmem_limit_bytes=VMEM_BYTES),
        name="last",
    )(b_matrix, c_matrix, mix, state, attn, dq, dk, dv, y, xg)


def build(mesh, n_z):
    n_seq, n_head = mesh.shape["seq"], mesh.shape["head"]
    tokens = P("seq", "head")
    whole = P("seq", None)
    return jax.shard_map(
        functools.partial(on_device, n_seq, n_head, n_z),
        mesh=mesh,
        in_specs=(
            tokens,
            tokens,
            tokens,
            tokens,
            tokens,
            whole,
            whole,
            tokens,
            P("head"),
            P("head"),
            tokens,
            P(),
        ),
        out_specs=(tokens, tokens, tokens, tokens, tokens, tokens, whole, whole),
        check_vma=False,
    )


def solution(mesh):
    return build(mesh, 8)
```

time: 216 us -> 60.1 us (0.28)
  the two profiles are of different devices: /device:TPU:8 before, /device:TPU:1 now
where the time goes in v1:
time: 60.1 us; the launch traced here: 59.7 us
  Pallas kernels  51.2 us (85%)
  local copies, waits for them, and re-layouts  7.78 us (13%)
  between operations  0.7 us (1%)
    pallas_call x1, Pallas kernels, on_device(): pl.pallas_call(functools.partial(main_kernel, n_seq, n_head, n_z), out_sh...  49.5 us
    unnamed x28, local copies, waits for them, and re-layouts  7.78 us
    pallas_call x1, Pallas kernels, on_device(): pl.pallas_call(functools.partial(last_kernel, n_head), out_shape=(wide, w...  1.79 us

profile of v1, /device:TPU:1, one launch (start us, length us, event | category | flops | bytes accessed | tf_op | source)
XLA Modules:
  0.0 59.7 jit_solution(2525492758123968564)
XLA Ops:
  0.6 0.0 copy-start.10
  0.6 0.0 copy-start.11
  0.7 0.0 copy-start.12
  0.7 0.0 copy-start.13
  0.7 0.6 %copy-done.10 = f32[256,2]{0,1:T(2,128)S(1)} copy-done((f32[256,2]{0,1:T(2,128)S(1)}, f32[256,2]{0,1:T(2,128)}, u32[]{:S(2)}) %copy-start.10) | copy-done | bytes 2072
  1.3 0.0 copy-done.11
  1.3 0.0 copy-done.12
  1.3 0.0 copy-done.13
  1.3 0.0 copy-start
  1.3 0.9 %copy-done = bf16[256,256]{1,0:T(8,128)(2,1)S(1)} copy-done((bf16[256,256]{1,0:T(8,128)(2,1)S(1)}, bf16[256,256]{1,0:T(8,128)(2,1)}, u32[]{:S(2)}) %copy-start) | copy-done | bytes 131096
  2.2 0.0 copy-start.2
  2.2 0.9 %copy-done.2 = bf16[256,256]{1,0:T(8,128)(2,1)S(1)} copy-done((bf16[256,256]{1,0:T(8,128)(2,1)S(1)}, bf16[256,256]{1,0:T(8,128)(2,1)}, u32[]{:S(2)}) %copy-start.2) | copy-done | bytes 131096
  3.2 0.0 copy-start.4
  3.2 0.9 %copy-done.4 = bf16[256,256]{1,0:T(8,128)(2,1)S(1)} copy-done((bf16[256,256]{1,0:T(8,128)(2,1)S(1)}, bf16[256,256]{1,0:T(8,128)(2,1)}, u32[]{:S(2)}) %copy-start.4) | copy-done | bytes 131096
  4.1 0.0 copy-start.5
  4.1 0.9 %copy-done.5 = bf16[256,256]{1,0:T(8,128)(2,1)S(1)} copy-done((bf16[256,256]{1,0:T(8,128)(2,1)S(1)}, bf16[256,256]{1,0:T(8,128)(2,1)}, u32[]{:S(2)}) %copy-start.5) | copy-done | bytes 131096
  5.0 0.0 copy-start.6
  5.0 0.9 %copy-done.6 = bf16[256,256]{1,0:T(8,128)(2,1)S(1)} copy-done((bf16[256,256]{1,0:T(8,128)(2,1)S(1)}, bf16[256,256]{1,0:T(8,128)(2,1)}, u32[]{:S(2)}) %copy-start.6) | copy-done | bytes 131096
  5.9 0.0 copy-start.7
  5.9 0.9 %copy-done.7 = bf16[256,256]{1,0:T(8,128)(2,1)S(1)} copy-done((bf16[256,256]{1,0:T(8,128)(2,1)S(1)}, bf16[256,256]{1,0:T(8,128)(2,1)}, u32[]{:S(2)}) %copy-start.7) | copy-done | bytes 131096
  6.8 0.0 copy-start.8
  6.8 0.8 %copy-done.8 = bf16[256,128]{1,0:T(8,128)(2,1)S(1)} copy-done((bf16[256,128]{1,0:T(8,128)(2,1)S(1)}, bf16[256,128]{1,0:T(8,128)(2,1)}, u32[]{:S(2)}) %copy-start.8) | copy-done | bytes 65560
  7.6 0.0 copy-start.9
  7.6 0.8 %copy-done.9 = bf16[256,128]{1,0:T(8,128)(2,1)S(1)} copy-done((bf16[256,128]{1,0:T(8,128)(2,1)S(1)}, bf16[256,128]{1,0:T(8,128)(2,1)}, u32[]{:S(2)}) %copy-start.9) | copy-done | bytes 65560
  8.4 0.0 copy-start.1
  8.5 0.0 copy-start.3
  8.5 49.5 %main.1 = (bf16[256,256]{1,0:T(8,128)(2,1)S(1)}, bf16[256,256]{1,0:T(8,128)(2,1)S(1)}, bf16[256,256]{1,0:T(8,128)(2,1)S(1)}, bf16[256,256]{1,0:T(8,128)(2,1)S(1)...) custom-call(f32[2]{0:T(128)S(1)} %copy-done.11, ...), custom_call_target="tpu_custom_call" | custom-call | tf_op jit(solution)/shard_map/main/pallas_call | solution.py:544
  57.9 0.0 copy-done.1
  57.9 0.0 copy-done.3
  57.9 1.8 %last.1 = (bf16[256,256]{1,0:T(8,128)(2,1)}, bf16[256,256]{1,0:T(8,128)(2,1)}, bf16[256,256]{1,0:T(8,128)(2,1)}, bf16[256,256]{1,0:T(8,128)(2,1)}, bf16[256,128]...) custom-call(bf16[256,256]{1,0:T(8,128)(2,1)S(1)} %copy-done.1, ...), custom_call_target="tpu_custom_call" | custom-call | tf_op jit(solution)/shard_map/last/pallas_call | solution.py:604
Async XLA Ops:
  0.6 0.7 %copy-start.10 = (f32[256,2]{0,1:T(2,128)S(1)}, f32[256,2]{0,1:T(2,128)}, u32[]{:S(2)}) copy-start(f32[256,2]{0,1:T(2,128)} %param.19) | copy-start | bytes 6148
  0.6 0.7 %copy-start.11 = (f32[2]{0:T(128)S(1)}, f32[2]{0:T(128)}, u32[]{:S(2)}) copy-start(f32[2]{0:T(128)} %rate_ref.1) | copy-start | bytes 28
  0.7 0.7 %copy-start.12 = (f32[2]{0:T(128)S(1)}, f32[2]{0:T(128)}, u32[]{:S(2)}) copy-start(f32[2]{0:T(128)} %gain_ref.1) | copy-start | bytes 28
  0.7 0.7 %copy-start.13 = (s32[128]{0:T(128)S(1)}, s32[128]{0:T(128)}, u32[]{:S(2)}) copy-start(s32[128]{0:T(128)} %param.23) | copy-start | bytes 1540
  1.3 0.9 %copy-start = (bf16[256,256]{1,0:T(8,128)(2,1)S(1)}, bf16[256,256]{1,0:T(8,128)(2,1)}, u32[]{:S(2)}) copy-start(bf16[256,256]{1,0:T(8,128)(2,1)} %b_ref.3) | copy-start | bytes 393220
  2.2 0.9 %copy-start.2 = (bf16[256,256]{1,0:T(8,128)(2,1)S(1)}, bf16[256,256]{1,0:T(8,128)(2,1)}, u32[]{:S(2)}) copy-start(bf16[256,256]{1,0:T(8,128)(2,1)} %c_ref.3) | copy-start | bytes 393220
  3.2 0.9 %copy-start.4 = (bf16[256,256]{1,0:T(8,128)(2,1)S(1)}, bf16[256,256]{1,0:T(8,128)(2,1)}, u32[]{:S(2)}) copy-start(bf16[256,256]{1,0:T(8,128)(2,1)} %q_ref.1) | copy-start | bytes 393220
  4.1 0.9 %copy-start.5 = (bf16[256,256]{1,0:T(8,128)(2,1)S(1)}, bf16[256,256]{1,0:T(8,128)(2,1)}, u32[]{:S(2)}) copy-start(bf16[256,256]{1,0:T(8,128)(2,1)} %k_ref.1) | copy-start | bytes 393220
  5.0 0.9 %copy-start.6 = (bf16[256,256]{1,0:T(8,128)(2,1)S(1)}, bf16[256,256]{1,0:T(8,128)(2,1)}, u32[]{:S(2)}) copy-start(bf16[256,256]{1,0:T(8,128)(2,1)} %v_ref.1) | copy-start | bytes 393220
  5.9 0.9 %copy-start.7 = (bf16[256,256]{1,0:T(8,128)(2,1)S(1)}, bf16[256,256]{1,0:T(8,128)(2,1)}, u32[]{:S(2)}) copy-start(bf16[256,256]{1,0:T(8,128)(2,1)} %do_ref.1) | copy-start | bytes 393220
  6.8 0.8 %copy-start.8 = (bf16[256,128]{1,0:T(8,128)(2,1)S(1)}, bf16[256,128]{1,0:T(8,128)(2,1)}, u32[]{:S(2)}) copy-start(bf16[256,128]{1,0:T(8,128)(2,1)} %x_ref.1) | copy-start | bytes 196612
  7.6 0.8 %copy-start.9 = (bf16[256,128]{1,0:T(8,128)(2,1)S(1)}, bf16[256,128]{1,0:T(8,128)(2,1)}, u32[]{:S(2)}) copy-start(bf16[256,128]{1,0:T(8,128)(2,1)} %g_ref.1) | copy-start | bytes 196612
  8.4 49.5 %copy-start.1 = (bf16[256,256]{1,0:T(8,128)(2,1)S(1)}, bf16[256,256]{1,0:T(8,128)(2,1)}, u32[]{:S(2)}) copy-start(bf16[256,256]{1,0:T(8,128)(2,1)} %b_ref.3) | copy-start | bytes 393220
  8.5 49.5 %copy-start.3 = (bf16[256,256]{1,0:T(8,128)(2,1)S(1)}, bf16[256,256]{1,0:T(8,128)(2,1)}, u32[]{:S(2)}) copy-start(bf16[256,256]{1,0:T(8,128)(2,1)} %c_ref.3) | copy-start | bytes 393220

commit v2 on v1

--- a/solution.py
+++ b/solution.py
@@ -13,7 +13,14 @@
 OFF = -1e30
 F32 = jnp.float32
 BF16 = jnp.bfloat16
-VMEM_BYTES = 40 * 1024 * 1024
+UNROLL = False
+NEAR_AT = 3
+VMEM_BYTES = 60 * 1024 * 1024
+
+
+def far_first(step, count):
+    odd = step % 2
+    return count // 2 + (step // 2 + odd) * (1 - 2 * odd)
 
 
 def dot(a, b):
@@ -65,6 +72,23 @@
     rate_ref,
     gain_ref,
     doc_ref,
+    dt_ref,
+    q_hbm,
+    k_hbm,
+    v_hbm,
+    do_hbm,
+    x_hbm,
+    g_hbm,
+    b_hbm,
+    c_hbm,
+    attn_ref,
+    dq_ref,
+    dk_ref,
+    dv_ref,
+    y_ref,
+    xg_ref,
+    mix_ref,
+    state_ref,
     q_ref,
     k_ref,
     v_ref,
@@ -73,15 +97,7 @@
     g_ref,
     b_ref,
     c_ref,
-    dt_ref,
-    attn_ref,
-    dq_ref,
-    dk_ref,
-    dv_ref,
-    y_ref,
-    xg_ref,
-    mix_ref,
-    state_ref,
+    load_sem,
     kv_in,
     qd_in,
     stat_out,
@@ -133,6 +149,24 @@
     def slot_of(index, count, side):
         return index + side * (count - 1 - 2 * index)
 
+    loads = [
+        pltpu.make_async_copy(source, target, load_sem.at[at])
+        for at, (source, target) in enumerate(
+            (
+                (x_hbm, x_ref),
+                (b_hbm, b_ref),
+                (g_hbm, g_ref),
+                (c_hbm, c_ref),
+                (q_hbm, q_ref),
+                (k_hbm, k_ref),
+                (v_hbm, v_ref),
+                (do_hbm, do_ref),
+            )
+        )
+    ]
+    for load in loads:
+        load.start()
+
     barrier = pltpu.get_barrier_semaphore()
 
     def greet(seq_index, head_index):
@@ -172,6 +206,8 @@
     source_weight = jnp.exp(-log_decay) * dt_wide
     last = log_decay[rows - 1 : rows, :]
     decay_all = jnp.exp(last)
+    for load in loads[:4]:
+        load.wait()
     mix_ref[hx, 0] = (carry_weight * g_ref[...].astype(F32)).astype(BF16)
     mix_ref[hx, 1] = (source_weight * x_ref[...].astype(F32)).astype(BF16)
     local_state = (decay_all * dot_tn(b_ref[...], mix_ref[hx, 1])).astype(BF16)
@@ -196,19 +232,19 @@
             ),
         )
 
-    def a_start(k, carry):
-        for copy in a_copies(k):
+    def a_start(step, carry):
+        for copy in a_copies(far_first(step, row)):
             copy.start()
         return carry
 
-    lax.fori_loop(1, row, a_start, 0)
+    lax.fori_loop(0, row - 1, a_start, 0, unroll=UNROLL)
     own_slot = slot_of(pos, row, core)
     a_dst[own_slot] = a_src[pos]
     la_dst[own_slot] = la_src[...]
 
     near = []
     for distance in (1, 2):
-        for part, (fore, back) in enumerate(((k_ref, q_ref), (v_ref, do_ref))):
+        for part, (fore, back) in enumerate(((k_hbm, q_hbm), (v_hbm, do_hbm))):
             at = (distance - 1) * 2 + part
             near.append(
                 pltpu.make_async_remote_copy(
@@ -230,8 +266,9 @@
                     MESH,
                 )
             )
-    for copy in near:
-        copy.start()
+    if NEAR_AT == 1:
+        for copy in near:
+            copy.start()
 
     def over_head(ref, send, recv):
         return [
@@ -243,7 +280,7 @@
                 (me, (hx + k) % n_head),
                 MESH,
             )
-            for k in range(1, n_head)
+            for k in [far_first(step, n_head) for step in range(n_head - 1)]
         ]
 
     def from_head(ref, send, recv):
@@ -276,6 +313,9 @@
         return carry
 
     lax.fori_loop(1, row, a_wait, 0)
+    if NEAR_AT == 2:
+        for copy in near:
+            copy.start()
 
     state = jnp.zeros((width, 128), F32)
     summed = jnp.zeros((1, 128), F32)
@@ -300,12 +340,15 @@
             ),
         )
 
-    def t_start(k, carry):
-        for copy in t_copies(k):
+    def t_start(step, carry):
+        for copy in t_copies(far_first(step, n_y)):
             copy.start()
         return carry
 
-    lax.fori_loop(1, n_y, t_start, 0)
+    lax.fori_loop(0, n_y - 1, t_start, 0, unroll=UNROLL)
+    if NEAR_AT == 3:
+        for copy in near:
+            copy.start()
     t_dst[own_group] = t_src[...]
     tl_dst[own_group] = tl_src[...]
 
@@ -341,13 +384,15 @@
             MESH,
         )
 
-    def r_start(k, carry):
-        r_copy(k).start()
-        return carry
-
-    lax.fori_loop(1, row, r_start, 0)
+    def r_start(step, carry):
+        r_copy(far_first(step, row)).start()
+        return carry
+
+    lax.fori_loop(0, row - 1, r_start, 0, unroll=UNROLL)
     r_dst[pos] = r_src[own_slot]
 
+    for load in loads[4:]:
+        load.wait()
     for copy in near:
         copy.wait_recv()
     columns = rows
@@ -544,9 +589,18 @@
     attn, dq, dk, dv, y, xg, mix, state = pl.pallas_call(
         functools.partial(main_kernel, n_seq, n_head, n_z),
         out_shape=(wide, wide, wide, wide, narrow, narrow, stacked, stacked),
-        in_specs=[smem, smem] + [vmem] * 10,
+        in_specs=[smem, smem] + [vmem] * 2 + [pl.BlockSpec(memory_space=pltpu.HBM)] * 8,
         out_specs=(vmem,) * 8,
         scratch_shapes=[
+            pltpu.VMEM((rows, columns), BF16),
+            pltpu.VMEM((rows, columns), BF16),
+            pltpu.VMEM((rows, columns), BF16),
+            pltpu.VMEM((rows, columns), BF16),
+            pltpu.VMEM((rows, 128), BF16),
+            pltpu.VMEM((rows, 128), BF16),
+            pltpu.VMEM((rows, b_matrix.shape[1]), BF16),
+            pltpu.VMEM((rows, b_matrix.shape[1]), BF16),
+            dma((8,)),
             pltpu.VMEM((2, 2, rows, columns), BF16),
             pltpu.VMEM((2, 2, rows, columns), BF16),
             pltpu.VMEM((8, rows), F32),
@@ -590,6 +644,7 @@
         decay_rates,
         skip_gain,
         doc_lengths.reshape(1, -1),
+        step_sizes.T,
         queries,
         key_rows,
         value_rows,
@@ -598,7 +653,6 @@
         ssm_out_grad,
         b_matrix,
         c_matrix,
-        step_sizes.T,
     )
     grads = jax.ShapeDtypeStruct((rows, b_matrix.shape[1]), F32)
     return pl.pallas_call(

time: 60.1 us -> 53.7 us (0.89)
  local copies, waits for them, and re-layouts: 7.78 us -> 0 us
  Pallas kernels: 51.2 us -> 52.9 us
    unnamed x28 -> x0, local copies, waits for them, and re-layouts: 7.78 us -> none
    pallas_call x1, Pallas kernels: 1.79 us -> 3.22 us  [on_device(): pl.pallas_call(functools.partial(last_kernel, n_head), out_shape=(wide, w...]
where the time goes in v2:
time: 53.7 us; the launch traced here: 53.5 us
  Pallas kernels  52.9 us (99%)
  between operations  0.64 us (1%)
    pallas_call x1, Pallas kernels, on_device(): pl.pallas_call(functools.partial(main_kernel, n_seq, n_head, n_z), out_sh...  49.6 us
    pallas_call x1, Pallas kernels, on_device(): pl.pallas_call(functools.partial(last_kernel, n_head), out_shape=(wide, w...  3.22 us

profile of v2, /device:TPU:1, one launch (start us, length us, event | category | flops | bytes accessed | tf_op | source)
XLA Modules:
  0.0 53.5 jit_solution(11630236367982608665)
XLA Ops:
  0.6 49.6 %main.1 = (bf16[256,256]{1,0:T(8,128)(2,1)}, bf16[256,256]{1,0:T(8,128)(2,1)}, bf16[256,256]{1,0:T(8,128)(2,1)}, bf16[256,256]{1,0:T(8,128)(2,1)}, bf16[256,128]...) custom-call(f32[2]{0:T(128)} %rate_ref.1, ...), custom_call_target="tpu_custom_call" | custom-call | tf_op jit(solution)/shard_map/main/pallas_call | solution.py:589
  50.3 3.2 %last.1 = (bf16[256,256]{1,0:T(8,128)(2,1)}, bf16[256,256]{1,0:T(8,128)(2,1)}, bf16[256,256]{1,0:T(8,128)(2,1)}, bf16[256,256]{1,0:T(8,128)(2,1)}, bf16[256,128]...) custom-call(bf16[256,256]{1,0:T(8,128)(2,1)} %b_ref.1, ...), custom_call_target="tpu_custom_call" | custom-call | tf_op jit(solution)/shard_map/last/pallas_call | solution.py:658

commit v3 on v2

--- a/solution.py
+++ b/solution.py
@@ -14,8 +14,8 @@
 F32 = jnp.float32
 BF16 = jnp.bfloat16
 UNROLL = False
-NEAR_AT = 3
-VMEM_BYTES = 60 * 1024 * 1024
+NEAR_AT = 1
+VMEM_BYTES = 40 * 1024 * 1024
 
 
 def far_first(step, count):
@@ -87,6 +87,8 @@
     dv_ref,
     y_ref,
     xg_ref,
+    bg_ref,
+    cg_ref,
     mix_ref,
     state_ref,
     q_ref,
@@ -113,7 +115,6 @@
     tl_src,
     tl_dst,
     r_src,
-    r_dst,
     near_send,
     near_recv,
     stat_send,
@@ -139,7 +140,7 @@
     n_y = n_seq // row
     rows = q_ref.shape[0]
     group, pos = me // row, me % row
-    core = pos % 2
+    chip, core = pos // 2, pos % 2
     base = group * row
     width = rows // n_z
 
@@ -242,55 +243,67 @@
     a_dst[own_slot] = a_src[pos]
     la_dst[own_slot] = la_src[...]
 
-    near = []
-    for distance in (1, 2):
-        for part, (fore, back) in enumerate(((k_hbm, q_hbm), (v_hbm, do_hbm))):
-            at = (distance - 1) * 2 + part
-            near.append(
-                pltpu.make_async_remote_copy(
-                    fore,
-                    kv_in.at[distance - 1, part],
-                    near_send.at[at],
-                    near_recv.at[at],
-                    (seq_at(distance), hx),
-                    MESH,
-                )
-            )
-            near.append(
-                pltpu.make_async_remote_copy(
-                    back,
-                    qd_in.at[distance - 1, part],
-                    near_send.at[4 + at],
-                    near_recv.at[4 + at],
-                    (seq_at(-distance), hx),
-                    MESH,
-                )
-            )
+    def near_copy(source, place, part, at, offset, sem):
+        return pltpu.make_async_remote_copy(
+            source,
+            place.at[at, part],
+            near_send.at[sem],
+            near_recv.at[(2 if place is qd_in else 0) + 4 * at + part],
+            (seq_at(offset), hx),
+            MESH,
+        )
+
+    keys_hbm, queries_hbm = (k_hbm, v_hbm), (q_hbm, do_hbm)
+    first_copies = [near_copy(keys_hbm[p], kv_in, p, 0, 1, p) for p in (0, 1)]
+    first_copies += [near_copy(queries_hbm[p], qd_in, p, 0, -1, 2 + p) for p in (0, 1)]
+    far_keys = [near_copy(keys_hbm[p], kv_in, p, 1, 2, 4 + p) for p in (0, 1)]
+    far_queries = [near_copy(queries_hbm[p], qd_in, p, 1, -2, 4 + p) for p in (0, 1)]
+    pass_keys = [near_copy(kv_in.at[0, p], kv_in, p, 1, 1, 6 + p) for p in (0, 1)]
+    pass_queries = [near_copy(qd_in.at[0, p], qd_in, p, 1, -1, 6 + p) for p in (0, 1)]
+
+    def near_start():
+        for copy in first_copies:
+            copy.start()
+
+        @pl.when(core == 0)
+        def _():
+            for copy in far_keys:
+                copy.start()
+
+        @pl.when(core == 1)
+        def _():
+            for copy in far_queries:
+                copy.start()
+
+    def near_pass():
+        for copy in first_copies:
+            copy.wait_recv()
+
+        @pl.when(core == 0)
+        def _():
+            for copy in pass_keys:
+                copy.start()
+
+        @pl.when(core == 1)
+        def _():
+            for copy in pass_queries:
+                copy.start()
+
     if NEAR_AT == 1:
-        for copy in near:
-            copy.start()
-
-    def over_head(ref, send, recv):
-        return [
-            pltpu.make_async_remote_copy(
-                ref.at[hx],
-                ref.at[hx],
-                send.at[k],
-                recv.at[hx],
-                (me, (hx + k) % n_head),
-                MESH,
-            )
-            for k in [far_first(step, n_head) for step in range(n_head - 1)]
-        ]
-
-    def from_head(ref, send, recv):
-        for k in range(1, n_head):
-            other = (hx + k) % n_head
-            pltpu.make_async_remote_copy(
-                ref.at[hx], ref.at[other], send.at[k], recv.at[other], (me, other), MESH
-            ).wait_recv()
-
-    mix_copies = over_head(mix_ref, mix_send, mix_recv)
+        near_start()
+
+    def mix_copy(k):
+        return pltpu.make_async_remote_copy(
+            mix_ref.at[hx],
+            mix_ref.at[hx],
+            mix_send.at[k],
+            mix_recv.at[hx],
+            (me, (hx + k) % n_head),
+            MESH,
+        )
+
+    head_steps = [far_first(step, n_head) for step in range(n_head - 1)]
+    mix_copies = [mix_copy(k) for k in head_steps]
     for copy in mix_copies:
         copy.start()
 
@@ -314,8 +327,7 @@
 
     lax.fori_loop(1, row, a_wait, 0)
     if NEAR_AT == 2:
-        for copy in near:
-            copy.start()
+        near_start()
 
     state = jnp.zeros((width, 128), F32)
     summed = jnp.zeros((1, 128), F32)
@@ -347,13 +359,14 @@
 
     lax.fori_loop(0, n_y - 1, t_start, 0, unroll=UNROLL)
     if NEAR_AT == 3:
-        for copy in near:
-            copy.start()
+        near_start()
     t_dst[own_group] = t_src[...]
     tl_dst[own_group] = tl_src[...]
 
     first = me * rows
     start_column = doc_start_column(doc_ref, first, rows)
+
+    near_pass()
 
     def t_wait(k, carry):
         slot = (own_group + k) % n_y
@@ -371,30 +384,71 @@
         grown = jnp.exp(tl_dst[slot]) * carried + t_dst[slot].astype(F32)
         carried = jnp.where(slot < own_group, grown, carried)
     for slot in range(row):
-        r_src[slot] = (scan_buf[slot] + jnp.exp(cum_buf[slot]) * carried).astype(BF16)
-
-    def r_copy(k):
-        other = (pos + k) % row
+        onward = jnp.where(core == 1, jnp.exp(la_dst[slot]), 1.0)
+        r_src[slot] = (onward * (scan_buf[slot] + jnp.exp(cum_buf[slot]) * carried)).astype(BF16)
+
+    def r_copy(other):
         return pltpu.make_async_remote_copy(
             r_src.at[slot_of(other, row, core)],
-            r_dst.at[pos],
-            r_send.at[k],
+            state_ref.at[hx, chip, core],
+            r_send.at[other],
             r_recv.at[pos],
             (base + other, hx),
             MESH,
         )
 
+    def r_arrival(other):
+        return pltpu.make_async_remote_copy(
+            r_src.at[0],
+            state_ref.at[hx, other // 2, other % 2],
+            r_send.at[other],
+            r_recv.at[other],
+            (base + other, hx),
+            MESH,
+        )
+
+    def near_first(step):
+        return (chip + n_z + (step + 1) // 2 * (2 * (step % 2) - 1)) % n_z
+
+    def x_copy(part, k):
+        return pltpu.make_async_remote_copy(
+            state_ref.at[hx, part],
+            state_ref.at[hx, part],
+            state_send.at[k, part],
+            state_recv.at[hx, part],
+            (me, (hx + k) % n_head),
+            MESH,
+        )
+
+    beside = 2 * chip + 1 - core
+    r_copy(beside).start()
+
     def r_start(step, carry):
-        r_copy(far_first(step, row)).start()
-        return carry
-
-    lax.fori_loop(0, row - 1, r_start, 0, unroll=UNROLL)
-    r_dst[pos] = r_src[own_slot]
+        for side in (0, 1):
+            r_copy(2 * near_first(step) + side).start()
+        return carry
+
+    lax.fori_loop(1, n_z, r_start, 0, unroll=UNROLL)
+    state_ref[hx, chip, core] = r_src[own_slot]
+
+    r_arrival(beside).wait_recv()
+    for k in head_steps:
+        x_copy(chip, k).start()
+
+    def r_pass(step, carry):
+        part = near_first(step)
+        for side in (0, 1):
+            r_arrival(2 * part + side).wait_recv()
+        for k in head_steps:
+            x_copy(part, k).start()
+        return carry
+
+    lax.fori_loop(1, n_z, r_pass, 0, unroll=UNROLL)
 
     for load in loads[4:]:
         load.wait()
-    for copy in near:
-        copy.wait_recv()
+    for part in (0, 1):
+        far_keys[part].wait_recv()
     columns = rows
     query_pos = (first + iota((rows, columns), 0)).astype(F32)
     start_wide = jnp.broadcast_to(start_column, (rows, columns))
@@ -445,64 +499,86 @@
     for copy in stat_copies:
         copy.start()
 
-    def r_wait(k, carry):
-        other = (pos + k) % row
-        pltpu.make_async_remote_copy(
-            r_src.at[0], r_dst.at[other], r_send.at[k], r_recv.at[other], (me, hx), MESH
-        ).wait_recv()
-        return carry
-
-    lax.fori_loop(1, row, r_wait, 0)
-    for z in range(n_z):
-        part = slice(z * width, (z + 1) * width)
-        state_ref[hx, 0, part, :] = r_dst[2 * z]
-        state_ref[hx, 1, part, :] = (decay_all * r_dst[2 * z + 1].astype(F32)).astype(BF16)
-    state_copies = over_head(state_ref, state_send, state_recv)
-    for copy in state_copies:
-        copy.start()
+    def entering(head, side):
+        return state_ref[head, :, side].reshape(rows, 128)
+
     y_ref[...] = (
-        carry_weight * (y_inner + dot(c_ref[...], state_ref[hx, 0]))
+        carry_weight * (y_inner + dot(c_ref[...], entering(hx, 0)))
         + gain_wide * x_ref[...].astype(F32)
     ).astype(BF16)
     xg_ref[...] = (
-        source_weight * (x_inner + dot(b_ref[...], state_ref[hx, 1]))
+        source_weight * (x_inner + dot(b_ref[...], entering(hx, 1)))
         + gain_wide * g_ref[...].astype(F32)
     ).astype(BF16)
-
-    for copy in stat_copies:
-        copy.wait_recv()
+    for k in head_steps:
+        other = (hx + k) % n_head
+        pltpu.make_async_remote_copy(
+            mix_ref.at[hx], mix_ref.at[other], mix_send.at[k], mix_recv.at[other], (me, other), MESH
+        ).wait_recv()
+    anti = iota((rows, rows), 0) <= iota((rows, rows), 1)
+    meet = sum(dot_nt(mix_ref[h, 0], mix_ref[h, 1]) for h in range(n_head))
+    cg_ref[...] = dot(jnp.where(causal, meet, 0.0).astype(BF16), b_ref[...])
+    meet = sum(dot_nt(mix_ref[h, 1], mix_ref[h, 0]) for h in range(n_head))
+    bg_ref[...] = dot(jnp.where(anti, meet, 0.0).astype(BF16), c_ref[...])
+
     key_pos = (first + iota((rows, columns), 0)).astype(F32)
-    turned = []
+    key_total, value_total = [0.0, 0.0], [0.0, 0.0]
     for distance in range(3):
+        if distance == 1:
+            for copy in stat_copies:
+                copy.wait_recv()
+            for part in (0, 1):
+                far_queries[part].wait_recv()
         stat = stat_out if distance == 0 else stat_in.at[distance - 1]
         query_pos = (seq_at(distance) * rows + iota((rows, columns), 1)).astype(F32)
-        turned.append((key_pos >= stat[4:5, :]) & (key_pos <= query_pos))
+        turned = (key_pos >= stat[4:5, :]) & (key_pos <= query_pos)
+        for h in range(2):
+            cols = slice(h * HEAD_DIM, (h + 1) * HEAD_DIM)
+            key, value = k_ref[:, cols], v_ref[:, cols]
+            if distance == 0:
+                query, grad = q_ref[:, cols], do_ref[:, cols]
+            else:
+                query, grad = qd_in[distance - 1, 0, :, cols], qd_in[distance - 1, 1, :, cols]
+            score = jnp.where(turned, dot_nt(key, query) * SCALE, OFF)
+            prob = jnp.exp(score - stat[h : h + 1, :])
+            value_total[h] = value_total[h] + dot(prob.astype(BF16), grad)
+            slope = prob * (dot_nt(value, grad) - stat[2 + h : 3 + h, :]) * SCALE
+            key_total[h] = key_total[h] + dot(slope.astype(BF16), query)
     for h in range(2):
         cols = slice(h * HEAD_DIM, (h + 1) * HEAD_DIM)
-        key, value = k_ref[:, cols], v_ref[:, cols]
-        key_total = value_total = jnp.zeros((rows, HEAD_DIM), F32)
-        for distance in range(3):
-            if distance == 0:
-                stat, query, grad = stat_out, q_ref[:, cols], do_ref[:, cols]
-            else:
-                stat = stat_in.at[distance - 1]
-                query, grad = qd_in[distance - 1, 0, :, cols], qd_in[distance - 1, 1, :, cols]
-            score = jnp.where(turned[distance], dot_nt(key, query) * SCALE, OFF)
-            prob = jnp.exp(score - stat[h : h + 1, :])
-            value_total = value_total + dot(prob.astype(BF16), grad)
-            slope = prob * (dot_nt(value, grad) - stat[2 + h : 3 + h, :]) * SCALE
-            key_total = key_total + dot(slope.astype(BF16), query)
-        dk_ref[:, cols] = key_total.astype(BF16)
-        dv_ref[:, cols] = value_total.astype(BF16)
-
-    from_head(mix_ref, mix_send, mix_recv)
-    from_head(state_ref, state_send, state_recv)
-
-    for copy in near + mix_copies + state_copies + stat_copies:
+        dk_ref[:, cols] = key_total[h].astype(BF16)
+        dv_ref[:, cols] = value_total[h].astype(BF16)
+    def x_wait(part, carry):
+        for k in head_steps:
+            other = (hx + k) % n_head
+            pltpu.make_async_remote_copy(
+                state_ref.at[hx, part],
+                state_ref.at[other, part],
+                state_send.at[k, part],
+                state_recv.at[other, part],
+                (me, other),
+                MESH,
+            ).wait_recv()
+        return carry
+
+    lax.fori_loop(0, n_z, x_wait, 0)
+    bg_ref[...] += sum(dot_nt(mix_ref[h, 1], entering(h, 1)) for h in range(n_head))
+    cg_ref[...] += sum(dot_nt(mix_ref[h, 0], entering(h, 0)) for h in range(n_head))
+    for copy in first_copies + mix_copies + stat_copies:
         copy.wait_send()
 
+    @pl.when(core == 0)
+    def _():
+        for copy in far_keys + pass_keys:
+            copy.wait_send()
+
+    @pl.when(core == 1)
+    def _():
+        for copy in far_queries + pass_queries:
+            copy.wait_send()
+
     def row_sent(k, carry):
-        for copy in (*a_copies(k), r_copy(k)):
+        for copy in (*a_copies(k), r_copy((pos + k) % row)):
             copy.wait_send()
         return carry
 
@@ -515,50 +591,23 @@
 
     lax.fori_loop(1, n_y, group_sent, 0)
 
-
-def last_kernel(
-    n_head,
-    b_ref,
-    c_ref,
-    mix_ref,
-    state_ref,
-    attn_in,
-    dq_in,
-    dk_in,
-    dv_in,
-    y_in,
-    xg_in,
-    attn_ref,
-    dq_ref,
-    dk_ref,
-    dv_ref,
-    y_ref,
-    xg_ref,
-    bg_ref,
-    cg_ref,
-):
-    rows = b_ref.shape[0]
-    causal = lower(rows)
-    anti = iota((rows, rows), 0) <= iota((rows, rows), 1)
-    meet = sum(dot_nt(mix_ref[h, 0], mix_ref[h, 1]) for h in range(n_head))
-    meet = jnp.where(causal, meet, 0.0).astype(BF16)
-    cg_ref[...] = dot(meet, b_ref[...]) + sum(
-        dot_nt(mix_ref[h, 0], state_ref[h, 0]) for h in range(n_head)
-    )
-    meet = sum(dot_nt(mix_ref[h, 1], mix_ref[h, 0]) for h in range(n_head))
-    meet = jnp.where(anti, meet, 0.0).astype(BF16)
-    bg_ref[...] = dot(meet, c_ref[...]) + sum(
-        dot_nt(mix_ref[h, 1], state_ref[h, 1]) for h in range(n_head)
-    )
-    for source, target in (
-        (attn_in, attn_ref),
-        (dq_in, dq_ref),
-        (dk_in, dk_ref),
-        (dv_in, dv_ref),
-        (y_in, y_ref),
-        (xg_in, xg_ref),
-    ):
-        target[...] = source[...]
+    def x_sent(part, carry):
+        for k in head_steps:
+            x_copy(part, k).wait_send()
+        return carry
+
+    lax.fori_loop(0, n_z, x_sent, 0)
+
+
+def last_kernel(*refs):
+    count = len(refs) // 2
+    copies = [
+        pltpu.make_async_copy(refs[n], refs[count + n], refs[-1].at[n]) for n in range(count)
+    ]
+    for copy in copies:
+        copy.start()
+    for copy in copies:
+        copy.wait()
 
 
 def on_device(
@@ -582,24 +631,27 @@
     row, n_y, width = 2 * n_z, n_seq // (2 * n_z), rows // n_z
     vmem = pl.BlockSpec(memory_space=pltpu.VMEM)
     smem = pl.BlockSpec(memory_space=pltpu.SMEM)
-    wide = jax.ShapeDtypeStruct((rows, columns), BF16)
-    narrow = jax.ShapeDtypeStruct((rows, 128), BF16)
-    stacked = jax.ShapeDtypeStruct((n_head, 2, rows, 128), BF16)
+    hbm = pl.BlockSpec(memory_space=pltpu.HBM)
+    states = b_matrix.shape[1]
+    shapes = ((rows, columns, BF16),) * 4 + ((rows, 128, BF16),) * 2 + ((rows, states, F32),) * 2
+    results = tuple(jax.ShapeDtypeStruct((m, n), kind) for m, n, kind in shapes)
     dma = pltpu.SemaphoreType.DMA
-    attn, dq, dk, dv, y, xg, mix, state = pl.pallas_call(
+    outs = pl.pallas_call(
         functools.partial(main_kernel, n_seq, n_head, n_z),
-        out_shape=(wide, wide, wide, wide, narrow, narrow, stacked, stacked),
-        in_specs=[smem, smem] + [vmem] * 2 + [pl.BlockSpec(memory_space=pltpu.HBM)] * 8,
+        out_shape=results,
+        in_specs=[smem, smem] + [vmem] * 2 + [hbm] * 8,
         out_specs=(vmem,) * 8,
         scratch_shapes=[
+            pltpu.VMEM((n_head, 2, rows, 128), BF16),
+            pltpu.VMEM((n_head, n_z, 2, width, 128), BF16),
             pltpu.VMEM((rows, columns), BF16),
             pltpu.VMEM((rows, columns), BF16),
             pltpu.VMEM((rows, columns), BF16),
             pltpu.VMEM((rows, columns), BF16),
             pltpu.VMEM((rows, 128), BF16),
             pltpu.VMEM((rows, 128), BF16),
-            pltpu.VMEM((rows, b_matrix.shape[1]), BF16),
-            pltpu.VMEM((rows, b_matrix.shape[1]), BF16),
+            pltpu.VMEM((rows, states), BF16),
+            pltpu.VMEM((rows, states), BF16),
             dma((8,)),
             pltpu.VMEM((2, 2, rows, columns), BF16),
             pltpu.VMEM((2, 2, rows, columns), BF16),
@@ -615,7 +667,6 @@
             pltpu.VMEM((n_y, width, 128), BF16),
             pltpu.VMEM((1, 128), F32),
             pltpu.VMEM((n_y, 1, 128), F32),
-            pltpu.VMEM((row, width, 128), BF16),
             pltpu.VMEM((row, width, 128), BF16),
             dma((8,)),
             dma((8,)),
@@ -633,8 +684,8 @@
             dma((row,)),
             dma((n_head,)),
             dma((n_head,)),
-            dma((n_head,)),
-            dma((n_head,)),
+            dma((n_head, n_z)),
+            dma((n_head, n_z)),
         ],
         compiler_params=pltpu.CompilerParams(
             collective_id=0, has_side_effects=True, vmem_limit_bytes=VMEM_BYTES
@@ -645,24 +696,29 @@
         skip_gain,
         doc_lengths.reshape(1, -1),
         step_sizes.T,
-        queries,
-        key_rows,
-        value_rows,
-        attn_out_grad,
-        ssm_input,
-        ssm_out_grad,
-        b_matrix,
-        c_matrix,
+        *[
+            pltpu.with_memory_space_constraint(array, pltpu.HBM)
+            for array in (
+                queries,
+                key_rows,
+                value_rows,
+                attn_out_grad,
+                ssm_input,
+                ssm_out_grad,
+                b_matrix,
+                c_matrix,
+            )
+        ],
     )
-    grads = jax.ShapeDtypeStruct((rows, b_matrix.shape[1]), F32)
     return pl.pallas_call(
-        functools.partial(last_kernel, n_head),
-        out_shape=(wide, wide, wide, wide, narrow, narrow, grads, grads),
-        in_specs=[vmem] * 10,
-        out_specs=(vmem,) * 8,
+        last_kernel,
+        out_shape=results,
+        in_specs=[vmem] * 8,
+        out_specs=(hbm,) * 8,
+        scratch_shapes=[dma((8,))],
         compiler_params=pltpu.CompilerParams(vmem_limit_bytes=VMEM_BYTES),
         name="last",
-    )(b_matrix, c_matrix, mix, state, attn, dq, dk, dv, y, xg)
+    )(*outs)
 
 
 def build(mesh, n_z):

time: 53.7 us -> 47 us (0.88)
  Pallas kernels: 52.9 us -> 45.5 us
  local copies, waits for them, and re-layouts: 0 us -> 0.67 us
    pallas_call x1, Pallas kernels: 49.6 us -> 44.4 us  [on_device(): pl.pallas_call(functools.partial(main_kernel, n_seq, n_head, n_z), out_sh...]
    pallas_call x1, Pallas kernels: 3.22 us -> 1.08 us  [on_device(): pl.pallas_call(last_kernel, out_shape=results, in_specs=[vmem] * 8, out_s...]
    unnamed x0 -> x8, local copies, waits for them, and re-layouts: none -> 0.67 us
where the time goes in v3:
time: 47 us; the launch traced here: 46.9 us
  Pallas kernels  45.5 us (97%)
  between operations  0.68 us (1%)
  local copies, waits for them, and re-layouts  0.67 us (1%)
    pallas_call x1, Pallas kernels, on_device(): pl.pallas_call(functools.partial(main_kernel, n_seq, n_head, n_z), out_sh...  44.4 us
    pallas_call x1, Pallas kernels, on_device(): pl.pallas_call(last_kernel, out_shape=results, in_specs=[vmem] * 8, out_s...  1.08 us

profile of v3, /device:TPU:1, one launch (start us, length us, event | category | flops | bytes accessed | tf_op | source)
XLA Modules:
  0.0 46.9 jit_solution(17361264592557200712)
XLA Ops:
  0.6 0.0 copy-start
  0.6 0.0 copy-start.1
  0.7 0.0 copy-start.2
  0.7 0.0 copy-start.3
  0.7 0.6 %copy-done = f32[256,2]{0,1:T(2,128)S(1)} copy-done((f32[256,2]{0,1:T(2,128)S(1)}, f32[256,2]{0,1:T(2,128)}, u32[]{:S(2)}) %copy-start) | copy-done | bytes 2072
  1.3 0.0 copy-done.1
  1.3 0.0 copy-done.2
  1.3 0.0 copy-done.3
  1.3 44.4 %main.1 = (bf16[256,256]{1,0:T(8,128)(2,1)S(1)}, bf16[256,256]{1,0:T(8,128)(2,1)S(1)}, bf16[256,256]{1,0:T(8,128)(2,1)S(1)}, bf16[256,256]{1,0:T(8,128)(2,1)S(1)...) custom-call(f32[2]{0:T(128)S(1)} %copy-done.1, ...), custom_call_target="tpu_custom_call" | custom-call | tf_op jit(solution)/shard_map/main/pallas_call | solution.py:639
  45.8 1.1 %last.1 = (bf16[256,256]{1,0:T(8,128)(2,1)}, bf16[256,256]{1,0:T(8,128)(2,1)}, bf16[256,256]{1,0:T(8,128)(2,1)}, bf16[256,256]{1,0:T(8,128)(2,1)}, bf16[256,128]...) custom-call(bf16[256,256]{1,0:T(8,128)(2,1)S(1)} %get-tuple-element.16.refs_0_, ...), custom_call_target="tpu_custom_call" | custom-call | tf_op jit(solution)/shard_map/last/pallas_call | solution.py:713
Async XLA Ops:
  0.6 0.7 %copy-start = (f32[256,2]{0,1:T(2,128)S(1)}, f32[256,2]{0,1:T(2,128)}, u32[]{:S(2)}) copy-start(f32[256,2]{0,1:T(2,128)} %param.19) | copy-start | bytes 6148
  0.6 0.7 %copy-start.1 = (f32[2]{0:T(128)S(1)}, f32[2]{0:T(128)}, u32[]{:S(2)}) copy-start(f32[2]{0:T(128)} %rate_ref.1) | copy-start | bytes 28
  0.7 0.7 %copy-start.2 = (f32[2]{0:T(128)S(1)}, f32[2]{0:T(128)}, u32[]{:S(2)}) copy-start(f32[2]{0:T(128)} %gain_ref.1) | copy-start | bytes 28
  0.7 0.7 %copy-start.3 = (s32[128]{0:T(128)S(1)}, s32[128]{0:T(128)}, u32[]{:S(2)}) copy-start(s32[128]{0:T(128)} %param.23) | copy-start | bytes 1540

commit v4 on v3

v4 whole, which is shorter than its diff:
```python
import functools

import jax
import jax.numpy as jnp
from jax import lax
from jax.experimental import pallas as pl
from jax.experimental.pallas import tpu as pltpu
from jax.sharding import PartitionSpec as P

MESH = pl.DeviceIdType.MESH
HEAD_DIM = 128
SCALE = HEAD_DIM**-0.5
OFF = -1e30
F32 = jnp.float32
BF16 = jnp.bfloat16
UNROLL = True
VMEM_BYTES = 40 * 1024 * 1024


def far_first(step, count):
    odd = step % 2
    return count // 2 + (step // 2 + odd) * (1 - 2 * odd)


def dot(a, b):
    return jnp.dot(a, b, preferred_element_type=F32)


def dot_nt(a, b):
    return lax.dot_general(a, b, (((1,), (1,)), ((), ())), preferred_element_type=F32)


def dot_tn(a, b):
    return lax.dot_general(a, b, (((0,), (0,)), ((), ())), preferred_element_type=F32)


def iota(shape, axis):
    return lax.broadcasted_iota(jnp.int32, shape, axis)


def lower(size):
    return iota((size, size), 1) <= iota((size, size), 0)


def doc_start_column(doc_ref, first, rows):
    docs = doc_ref.shape[1]
    lengths = jnp.broadcast_to(doc_ref[...], (16, docs))
    upper = jnp.where(iota((docs, docs), 0) <= iota((docs, docs), 1), 1.0, 0.0).astype(BF16)
    high, low = lengths // 16, lengths % 16
    ends = 16.0 * dot(high.astype(F32).astype(BF16), upper) + dot(
        low.astype(F32).astype(BF16), upper
    )
    ends = jnp.broadcast_to(ends[0:1, :], (rows, docs))
    position = (first + iota((rows, docs), 0)).astype(F32)
    return jnp.max(jnp.where(ends <= position, ends, 0.0), axis=1, keepdims=True)


def running_sum(rows):
    ones = jnp.where(lower(rows.shape[0]), 1.0, 0.0).astype(BF16)
    high = rows.astype(BF16)
    rest = rows - high.astype(F32)
    middle = rest.astype(BF16)
    low = (rest - middle.astype(F32)).astype(BF16)
    return dot(ones, high) + dot(ones, middle) + dot(ones, low)


def main_kernel(
    n_seq,
    n_head,
    n_z,
    rate_hbm,
    gain_hbm,
    doc_hbm,
    dt_hbm,
    q_hbm,
    k_hbm,
    v_hbm,
    do_hbm,
    x_hbm,
    g_hbm,
    b_hbm,
    c_hbm,
    attn_ref,
    dq_ref,
    dk_ref,
    dv_ref,
    y_ref,
    xg_ref,
    bg_ref,
    cg_ref,
    mix_ref,
    state_ref,
    q_ref,
    k_ref,
    v_ref,
    do_ref,
    x_ref,
    g_ref,
    b_ref,
    c_ref,
    rate_ref,
    gain_ref,
    doc_ref,
    dt_ref,
    load_sem,
    kv_in,
    qd_in,
    stat_out,
    stat_in,
    a_src,
    a_dst,
    la_src,
    la_dst,
    scan_buf,
    cum_buf,
    t_src,
    t_dst,
    tl_src,
    tl_dst,
    r_src,
    near_send,
    near_recv,
    stat_send,
    stat_recv,
    a_send,
    a_recv,
    la_send,
    la_recv,
    t_send,
    t_recv,
    tl_send,
    tl_recv,
    r_send,
    r_recv,
    mix_send,
    mix_recv,
    state_send,
    state_recv,
):
    me = lax.axis_index("seq")
    hx = lax.axis_index("head")
    row = 2 * n_z
    n_y = n_seq // row
    rows = q_ref.shape[0]
    group, pos = me // row, me % row
    chip, core = pos // 2, pos % 2
    base = group * row
    width = rows // n_z

    def seq_at(offset):
        return (me + offset + n_seq) % n_seq

    def wait_all(buffer, count, sem):
        blocks = buffer.at[pl.ds(0, count)]
        pltpu.make_async_copy(blocks, blocks, sem).wait()

    def slot_of(index, count, side):
        return index + side * (count - 1 - 2 * index)

    loads = [
        pltpu.make_async_copy(source, target, load_sem.at[at])
        for at, (source, target) in enumerate(
            (
                (dt_hbm, dt_ref),
                (rate_hbm, rate_ref),
                (gain_hbm, gain_ref),
                (x_hbm, x_ref),
                (b_hbm, b_ref),
                (g_hbm, g_ref),
                (c_hbm, c_ref),
                (q_hbm, q_ref),
                (k_hbm, k_ref),
                (v_hbm, v_ref),
                (do_hbm, do_ref),
                (doc_hbm, doc_ref),
            )
        )
    ]
    for load in loads:
        load.start()

    barrier = pltpu.get_barrier_semaphore()

    def greet(seq_index, head_index):
        pl.semaphore_signal(
            barrier, inc=1, device_id=(seq_index, head_index), device_id_type=MESH
        )

    for offset in (-2, -1, 1, 2):
        greet(seq_at(offset), hx)

    def greet_row(k, carry):
        greet(base + (pos + k) % row, hx)
        return carry

    lax.fori_loop(1, row, greet_row, 0)

    def greet_group(k, carry):
        greet(((group + k) % n_y) * row + pos, hx)
        return carry

    lax.fori_loop(1, n_y, greet_group, 0)
    for k in range(1, n_head):
        greet(me, (hx + k) % n_head)

    for load in loads[:3]:
        load.wait()
    lanes_low = iota((rows, 128), 1) < 64
    dt_wide = jnp.concatenate(
        [
            jnp.broadcast_to(dt_ref[0:1, :], (64, rows)),
            jnp.broadcast_to(dt_ref[1:2, :], (64, rows)),
        ],
        axis=0,
    ).T
    rate_wide = jnp.where(lanes_low, rate_ref[0], rate_ref[1])
    gain_wide = jnp.where(lanes_low, gain_ref[0], gain_ref[1])
    log_decay = running_sum(-dt_wide * rate_wide)
    carry_weight = jnp.exp(log_decay)
    source_weight = jnp.exp(-log_decay) * dt_wide
    last = log_decay[rows - 1 : rows, :]
    decay_all = jnp.exp(last)
    for load in loads[3:7]:
        load.wait()
    mix_ref[hx, 0] = (carry_weight * g_ref[...].astype(F32)).astype(BF16)
    mix_ref[hx, 1] = (source_weight * x_ref[...].astype(F32)).astype(BF16)
    local_state = (decay_all * dot_tn(b_ref[...], mix_ref[hx, 1])).astype(BF16)
    local_adjoint = dot_tn(c_ref[...], mix_ref[hx, 0]).astype(BF16)
    for z in range(n_z):
        a_src[2 * z] = local_state[z * width : (z + 1) * width, :]
        a_src[2 * z + 1] = local_adjoint[z * width : (z + 1) * width, :]
    la_src[...] = last

    pl.semaphore_wait(barrier, 4 + (row - 1) + (n_y - 1) + (n_head - 1))

    def a_copies(k):
        owner = (pos + k) % row
        slot = slot_of(pos, row, owner % 2)
        target = (base + owner, hx)
        return (
            pltpu.make_async_remote_copy(
                a_src.at[owner], a_dst.at[slot], a_send.at[0], a_recv.at[0], target, MESH
            ),
            pltpu.make_async_remote_copy(
                la_src, la_dst.at[slot], la_send.at[0], la_recv.at[0], target, MESH
            ),
        )

    def a_start(step, carry):
        for copy in a_copies(far_first(step, row)):
            copy.start()
        return carry

    lax.fori_loop(0, row - 1, a_start, 0, unroll=UNROLL)
    own_slot = slot_of(pos, row, core)
    a_dst[own_slot] = a_src[pos]
    la_dst[own_slot] = la_src[...]

    def near_copy(source, place, part, at, offset, sem):
        return pltpu.make_async_remote_copy(
            source,
            place.at[at, part],
            near_send.at[sem],
            near_recv.at[(2 if place is qd_in else 0) + 4 * at + part],
            (seq_at(offset), hx),
            MESH,
        )

    keys_hbm, queries_hbm = (k_hbm, v_hbm), (q_hbm, do_hbm)
    first_copies = [near_copy(keys_hbm[p], kv_in, p, 0, 1, p) for p in (0, 1)]
    first_copies += [near_copy(queries_hbm[p], qd_in, p, 0, -1, 2 + p) for p in (0, 1)]
    far_keys = [near_copy(keys_hbm[p], kv_in, p, 1, 2, 4 + p) for p in (0, 1)]
    far_queries = [near_copy(queries_hbm[p], qd_in, p, 1, -2, 4 + p) for p in (0, 1)]
    pass_keys = [near_copy(kv_in.at[0, p], kv_in, p, 1, 1, 6 + p) for p in (0, 1)]
    pass_queries = [near_copy(qd_in.at[0, p], qd_in, p, 1, -1, 6 + p) for p in (0, 1)]

    def near_start():
        for copy in first_copies:
            copy.start()

        @pl.when(core == 0)
        def _():
            for copy in far_keys:
                copy.start()

        @pl.when(core == 1)
        def _():
            for copy in far_queries:
                copy.start()

    def relay(arriving, onward):
        for copy, passed in zip(arriving, onward):
            copy.wait_recv()
            passed.start()

    def mix_copy(k):
        return pltpu.make_async_remote_copy(
            mix_ref.at[hx],
            mix_ref.at[hx],
            mix_send.at[k],
            mix_recv.at[hx],
            (me, (hx + k) % n_head),
            MESH,
        )

    head_steps = [far_first(step, n_head) for step in range(n_head - 1)]
    mix_copies = [mix_copy(k) for k in head_steps]
    for copy in mix_copies:
        copy.start()

    causal = lower(rows)
    meet = jnp.where(causal, dot_nt(c_ref[...], b_ref[...]), 0.0).astype(BF16)
    y_inner = dot(meet, mix_ref[hx, 1])
    meet_back = jnp.where(
        iota((rows, rows), 0) <= iota((rows, rows), 1), dot_nt(b_ref[...], c_ref[...]), 0.0
    ).astype(BF16)
    x_inner = dot(meet_back, mix_ref[hx, 0])

    wait_all(a_dst, row - 1, a_recv.at[0])
    wait_all(la_dst, row - 1, la_recv.at[0])

    state = jnp.zeros((width, 128), F32)
    summed = jnp.zeros((1, 128), F32)
    for slot in range(row):
        scan_buf[slot] = state
        cum_buf[slot] = summed
        state = jnp.exp(la_dst[slot]) * state + a_dst[slot].astype(F32)
        summed = summed + la_dst[slot]
    t_src[...] = state.astype(BF16)
    tl_src[...] = summed

    own_group = slot_of(group, n_y, core)

    def t_copies(k):
        target = (((group + k) % n_y) * row + pos, hx)
        return (
            pltpu.make_async_remote_copy(
                t_src, t_dst.at[own_group], t_send.at[0], t_recv.at[0], target, MESH
            ),
            pltpu.make_async_remote_copy(
                tl_src, tl_dst.at[own_group], tl_send.at[0], tl_recv.at[0], target, MESH
            ),
        )

    def t_start(step, carry):
        for copy in t_copies(far_first(step, n_y)):
            copy.start()
        return carry

    lax.fori_loop(0, n_y - 1, t_start, 0, unroll=UNROLL)
    near_start()
    t_dst[own_group] = t_src[...]
    tl_dst[own_group] = tl_src[...]

    first = me * rows
    loads[11].wait()
    start_column = doc_start_column(doc_ref, first, rows)

    columns = rows
    stat_copies = [
        pltpu.make_async_remote_copy(
            stat_out,
            stat_in.at[distance - 1],
            stat_send.at[distance - 1],
            stat_recv.at[distance - 1],
            (seq_at(-distance), hx),
            MESH,
        )
        for distance in (1, 2)
    ]

    def forward():
        for load in loads[7:11]:
            load.wait()
        @pl.when(core == 1)
        def _():
            for copy in first_copies[:2]:
                copy.wait_recv()

        for part in (0, 1):
            far_keys[part].wait_recv()
        query_pos = (first + iota((rows, columns), 0)).astype(F32)
        start_wide = jnp.broadcast_to(start_column, (rows, columns))
        masks = []
        for distance in range(3):
            key_pos = (first - distance * rows + iota((rows, columns), 1)).astype(F32)
            masks.append((key_pos >= start_wide) & (key_pos <= query_pos))
        lane = iota((rows, 128), 1)
        stats = jnp.where(lane == 4, start_column, 0.0)
        for h in range(2):
            cols = slice(h * HEAD_DIM, (h + 1) * HEAD_DIM)
            query, grad = q_ref[:, cols], do_ref[:, cols]
            keys = [k_ref[:, cols], kv_in[0, 0, :, cols], kv_in[1, 0, :, cols]]
            values = [v_ref[:, cols], kv_in[0, 1, :, cols], kv_in[1, 1, :, cols]]
            scores = [
                jnp.where(mask, dot_nt(query, key) * SCALE, OFF) for mask, key in zip(masks, keys)
            ]
            top = jnp.max(
                jnp.maximum(jnp.maximum(scores[0], scores[1]), scores[2]), axis=1, keepdims=True
            )
            powers = [jnp.exp(score - top) for score in scores]
            total = jnp.sum(powers[0] + powers[1] + powers[2], axis=1, keepdims=True)
            inverse = 1.0 / total
            probs = [power * inverse for power in powers]
            out = sum(dot(prob.astype(BF16), value) for prob, value in zip(probs, values))
            out = out.astype(BF16)
            attn_ref[:, cols] = out
            delta = jnp.sum(grad.astype(F32) * out.astype(F32), axis=1, keepdims=True)
            slopes = [
                (prob * (dot_nt(grad, value) - delta) * SCALE).astype(BF16)
                for prob, value in zip(probs, values)
            ]
            dq_ref[:, cols] = sum(dot(slope, key) for slope, key in zip(slopes, keys)).astype(BF16)
            stats = jnp.where(lane == h, top + jnp.log(total), stats)
            stats = jnp.where(lane == 2 + h, delta, stats)
        stat_out[...] = stats.T[0:8, :]
        for copy in stat_copies:
            copy.start()

    def inner():
        for k in head_steps:
            other = (hx + k) % n_head
            pltpu.make_async_remote_copy(
                mix_ref.at[hx], mix_ref.at[other], mix_send.at[k], mix_recv.at[other], (me, other), MESH
            ).wait_recv()
        anti = iota((rows, rows), 0) <= iota((rows, rows), 1)
        meet = sum(dot_nt(mix_ref[h, 0], mix_ref[h, 1]) for h in range(n_head))
        cg_ref[...] = dot(jnp.where(causal, meet, 0.0).astype(BF16), b_ref[...])
        meet = sum(dot_nt(mix_ref[h, 1], mix_ref[h, 0]) for h in range(n_head))
        bg_ref[...] = dot(jnp.where(anti, meet, 0.0).astype(BF16), c_ref[...])

    def backward():
        key_pos = (first + iota((rows, columns), 0)).astype(F32)
        key_total, value_total = [0.0, 0.0], [0.0, 0.0]
        for distance in range(3):
            if distance == 1:
                for copy in stat_copies:
                    copy.wait_recv()


                @pl.when(core == 0)
                def _():
                    for copy in first_copies[2:]:
                        copy.wait_recv()

                for part in (0, 1):
                    far_queries[part].wait_recv()
            stat = stat_out if distance == 0 else stat_in.at[distance - 1]
            query_pos = (seq_at(distance) * rows + iota((rows, columns), 1)).astype(F32)
            turned = (key_pos >= stat[4:5, :]) & (key_pos <= query_pos)
            for h in range(2):
                cols = slice(h * HEAD_DIM, (h + 1) * HEAD_DIM)
                key, value = k_ref[:, cols], v_ref[:, cols]
                if distance == 0:
                    query, grad = q_ref[:, cols], do_ref[:, cols]
                else:
                    query, grad = qd_in[distance - 1, 0, :, cols], qd_in[distance - 1, 1, :, cols]
                score = jnp.where(turned, dot_nt(key, query) * SCALE, OFF)
                prob = jnp.exp(score - stat[h : h + 1, :])
                value_total[h] = value_total[h] + dot(prob.astype(BF16), grad)
                slope = prob * (dot_nt(value, grad) - stat[2 + h : 3 + h, :]) * SCALE
                key_total[h] = key_total[h] + dot(slope.astype(BF16), query)
        for h in range(2):
            cols = slice(h * HEAD_DIM, (h + 1) * HEAD_DIM)
            dk_ref[:, cols] = key_total[h].astype(BF16)
            dv_ref[:, cols] = value_total[h].astype(BF16)


    wait_all(t_dst, n_y - 1, t_recv.at[0])
    wait_all(tl_dst, n_y - 1, tl_recv.at[0])
    carried = jnp.zeros((width, 128), F32)
    for slot in range(n_y):
        grown = jnp.exp(tl_dst[slot]) * carried + t_dst[slot].astype(F32)
        carried = jnp.where(slot < own_group, grown, carried)
    for slot in range(row):
        onward = jnp.where(core == 1, jnp.exp(la_dst[slot]), 1.0)
        r_src[slot] = (onward * (scan_buf[slot] + jnp.exp(cum_buf[slot]) * carried)).astype(BF16)

    def r_copy(other):
        return pltpu.make_async_remote_copy(
            r_src.at[slot_of(other, row, core)],
            state_ref.at[hx, chip, core],
            r_send.at[0],
            r_recv.at[pos],
            (base + other, hx),
            MESH,
        )

    def r_arrival(other):
        return pltpu.make_async_remote_copy(
            r_src.at[0],
            state_ref.at[hx, other // 2, other % 2],
            r_send.at[0],
            r_recv.at[other],
            (base + other, hx),
            MESH,
        )

    def near_first(step):
        return (chip + n_z + (step + 1) // 2 * (2 * (step % 2) - 1)) % n_z

    def x_copy(part, k):
        return pltpu.make_async_remote_copy(
            state_ref.at[hx, part],
            state_ref.at[hx, part],
            state_send.at[k],
            state_recv.at[hx],
            (me, (hx + k) % n_head),
            MESH,
        )

    beside = 2 * chip + 1 - core
    r_copy(beside).start()

    def r_start(step, carry):
        for side in (0, 1):
            r_copy(2 * near_first(step) + side).start()
        return carry

    lax.fori_loop(1, n_z, r_start, 0, unroll=UNROLL)
    state_ref[hx, chip, core] = r_src[own_slot]

    r_arrival(beside).wait_recv()
    for k in head_steps:
        x_copy(chip, k).start()

    def r_pass(step, carry):
        part = near_first(step)
        for side in (0, 1):
            r_arrival(2 * part + side).wait_recv()
        for k in head_steps:
            x_copy(part, k).start()
        return carry

    lax.fori_loop(1, n_z, r_pass, 0, unroll=UNROLL)

    pl.when(core == 0)(lambda: relay(first_copies[:2], pass_keys))
    pl.when(core == 1)(lambda: relay(first_copies[2:], pass_queries))
    forward()
    def entering(head, side):
        return state_ref[head, :, side].reshape(rows, 128)

    y_ref[...] = (
        carry_weight * (y_inner + dot(c_ref[...], entering(hx, 0)))
        + gain_wide * x_ref[...].astype(F32)
    ).astype(BF16)
    xg_ref[...] = (
        source_weight * (x_inner + dot(b_ref[...], entering(hx, 1)))
        + gain_wide * g_ref[...].astype(F32)
    ).astype(BF16)
    inner()
    backward()

    for copy in first_copies + mix_copies + stat_copies:
        copy.wait_send()

    @pl.when(core == 0)
    def _():
        for copy in far_keys + pass_keys:
            copy.wait_send()

    @pl.when(core == 1)
    def _():
        for copy in far_queries + pass_queries:
            copy.wait_send()

    wait_all(a_src, row - 1, a_send.at[0])
    wait_all(la_dst, row - 1, la_send.at[0])
    wait_all(t_dst, n_y - 1, t_send.at[0])
    wait_all(tl_dst, n_y - 1, tl_send.at[0])
    wait_all(r_src, row - 1, r_send.at[0])

    for k in head_steps:
        wait_all(state_ref.at[hx], n_z, state_send.at[k])
    for k in head_steps:
        other = (hx + k) % n_head
        wait_all(state_ref.at[other], n_z, state_recv.at[other])
    bg_ref[...] += sum(dot_nt(mix_ref[h, 1], entering(h, 1)) for h in range(n_head))
    cg_ref[...] += sum(dot_nt(mix_ref[h, 0], entering(h, 0)) for h in range(n_head))


def last_kernel(*refs):
    count = len(refs) // 2
    copies = [
        pltpu.make_async_copy(refs[n], refs[count + n], refs[-1].at[n]) for n in range(count)
    ]
    for copy in copies:
        copy.start()
    for copy in copies:
        copy.wait()


def on_device(
    n_seq,
    n_head,
    n_z,
    queries,
    key_rows,
    value_rows,
    attn_out_grad,
    ssm_input,
    b_matrix,
    c_matrix,
    step_sizes,
    decay_rates,
    skip_gain,
    ssm_out_grad,
    doc_lengths,
):
    rows, columns = queries.shape
    row, n_y, width = 2 * n_z, n_seq // (2 * n_z), rows // n_z
    vmem = pl.BlockSpec(memory_space=pltpu.VMEM)
    hbm = pl.BlockSpec(memory_space=pltpu.HBM)
    states = b_matrix.shape[1]
    shapes = ((rows, columns, BF16),) * 4 + ((rows, 128, BF16),) * 2 + ((rows, states, F32),) * 2
    results = tuple(jax.ShapeDtypeStruct((m, n), kind) for m, n, kind in shapes)
    dma = pltpu.SemaphoreType.DMA
    outs = pl.pallas_call(
        functools.partial(main_kernel, n_seq, n_head, n_z),
        out_shape=results,
        in_specs=[hbm] * 12,
        out_specs=(vmem,) * 8,
        scratch_shapes=[
            pltpu.VMEM((n_head, 2, rows, 128), BF16),
            pltpu.VMEM((n_head, n_z, 2, width, 128), BF16),
            pltpu.VMEM((rows, columns), BF16),
            pltpu.VMEM((rows, columns), BF16),
            pltpu.VMEM((rows, columns), BF16),
            pltpu.VMEM((rows, columns), BF16),
            pltpu.VMEM((rows, 128), BF16),
            pltpu.VMEM((rows, 128), BF16),
            pltpu.VMEM((rows, states), BF16),
            pltpu.VMEM((rows, states), BF16),
            pltpu.SMEM(decay_rates.shape, F32),
            pltpu.SMEM(skip_gain.shape, F32),
            pltpu.VMEM((1, doc_lengths.shape[0]), jnp.int32),
            pltpu.VMEM((step_sizes.shape[1], rows), F32),
            dma((12,)),
            pltpu.VMEM((2, 2, rows, columns), BF16),
            pltpu.VMEM((2, 2, rows, columns), BF16),
            pltpu.VMEM((8, rows), F32),
            pltpu.VMEM((2, 8, rows), F32),
            pltpu.VMEM((row, width, 128), BF16),
            pltpu.VMEM((row, width, 128), BF16),
            pltpu.VMEM((1, 128), F32),
            pltpu.VMEM((row, 1, 128), F32),
            pltpu.VMEM((row, width, 128), F32),
            pltpu.VMEM((row, 1, 128), F32),
            pltpu.VMEM((width, 128), BF16),
            pltpu.VMEM((n_y, width, 128), BF16),
            pltpu.VMEM((1, 128), F32),
            pltpu.VMEM((n_y, 1, 128), F32),
            pltpu.VMEM((row, width, 128), BF16),
            dma((8,)),
            dma((8,)),
            dma((2,)),
            dma((2,)),
            *[dma((1,))] * 9,
            dma((row,)),
            dma((n_head,)),
            dma((n_head,)),
            dma((n_head,)),
            dma((n_head,)),
        ],
        compiler_params=pltpu.CompilerParams(
            collective_id=0, has_side_effects=True, vmem_limit_bytes=VMEM_BYTES
        ),
        name="main",
    )(
        *[
            pltpu.with_memory_space_constraint(array, pltpu.HBM)
            for array in (
                decay_rates,
                skip_gain,
                doc_lengths.reshape(1, -1),
                step_sizes.T,
                queries,
                key_rows,
                value_rows,
                attn_out_grad,
                ssm_input,
                ssm_out_grad,
                b_matrix,
                c_matrix,
            )
        ],
    )
    return pl.pallas_call(
        last_kernel,
        out_shape=results,
        in_specs=[vmem] * 8,
        out_specs=(hbm,) * 8,
        scratch_shapes=[dma((8,))],
        compiler_params=pltpu.CompilerParams(vmem_limit_bytes=VMEM_BYTES),
        name="last",
    )(*outs)


def build(mesh, n_z):
    n_seq, n_head = mesh.shape["seq"], mesh.shape["head"]
    tokens = P("seq", "head")
    whole = P("seq", None)
    return jax.shard_map(
        functools.partial(on_device, n_seq, n_head, n_z),
        mesh=mesh,
        in_specs=(
            tokens,
            tokens,
            tokens,
            tokens,
            tokens,
            whole,
            whole,
            tokens,
            P("head"),
            P("head"),
            tokens,
            P(),
        ),
        out_specs=(tokens, tokens, tokens, tokens, tokens, tokens, whole, whole),
        check_vma=False,
    )


def solution(mesh):
    return build(mesh, 8)
```

time: 47 us -> 42.9 us (0.913)
  Pallas kernels: 45.5 us -> 42.2 us
  local copies, waits for them, and re-layouts: 0.67 us -> 0 us
    pallas_call x1, Pallas kernels: 44.4 us -> 41.1 us  [on_device(): pl.pallas_call(functools.partial(main_kernel, n_seq, n_head, n_z), out_sh...]
    unnamed x8 -> x0, local copies, waits for them, and re-layouts: 0.67 us -> none
where the time goes in v4:
time: 42.9 us; the launch traced here: 42.8 us
  Pallas kernels  42.2 us (98%)
  between operations  0.65 us (2%)
    pallas_call x1, Pallas kernels, on_device(): pl.pallas_call(functools.partial(main_kernel, n_seq, n_head, n_z), out_sh...  41.1 us
    pallas_call x1, Pallas kernels, on_device(): pl.pallas_call(last_kernel, out_shape=results, in_specs=[vmem] * 8, out_s...  1.08 us

profile of v4, /device:TPU:1, one launch (start us, length us, event | category | flops | bytes accessed | tf_op | source)
XLA Modules:
  0.0 42.8 jit_solution(2381188154930526015)
XLA Ops:
  0.6 41.1 %main.1 = (bf16[256,256]{1,0:T(8,128)(2,1)S(1)}, bf16[256,256]{1,0:T(8,128)(2,1)S(1)}, bf16[256,256]{1,0:T(8,128)(2,1)S(1)}, bf16[256,256]{1,0:T(8,128)(2,1)S(1)...) custom-call(f32[2]{0:T(128)} %rate_hbm.1, ...), custom_call_target="tpu_custom_call" | custom-call | tf_op jit(solution)/shard_map/main/pallas_call | solution.py:618
  41.7 1.1 %last.1 = (bf16[256,256]{1,0:T(8,128)(2,1)}, bf16[256,256]{1,0:T(8,128)(2,1)}, bf16[256,256]{1,0:T(8,128)(2,1)}, bf16[256,256]{1,0:T(8,128)(2,1)}, bf16[256,128]...) custom-call(bf16[256,256]{1,0:T(8,128)(2,1)S(1)} %get-tuple-element.16.refs_0_, ...), custom_call_target="tpu_custom_call" | custom-call | tf_op jit(solution)/shard_map/last/pallas_call | solution.py:688

commit v5 on v4

--- a/solution.py
+++ b/solution.py
@@ -193,13 +193,13 @@
         greet(base + (pos + k) % row, hx)
         return carry
 
-    lax.fori_loop(1, row, greet_row, 0)
+    lax.fori_loop(1, row, greet_row, 0, unroll=True)
 
     def greet_group(k, carry):
         greet(((group + k) % n_y) * row + pos, hx)
         return carry
 
-    lax.fori_loop(1, n_y, greet_group, 0)
+    lax.fori_loop(1, n_y, greet_group, 0, unroll=True)
     for k in range(1, n_head):
         greet(me, (hx + k) % n_head)
 
@@ -305,9 +305,6 @@
 
     head_steps = [far_first(step, n_head) for step in range(n_head - 1)]
     mix_copies = [mix_copy(k) for k in head_steps]
-    for copy in mix_copies:
-        copy.start()
-
     causal = lower(rows)
     meet = jnp.where(causal, dot_nt(c_ref[...], b_ref[...]), 0.0).astype(BF16)
     y_inner = dot(meet, mix_ref[hx, 1])
@@ -349,6 +346,8 @@
 
     lax.fori_loop(0, n_y - 1, t_start, 0, unroll=UNROLL)
     near_start()
+    for copy in mix_copies:
+        copy.start()
     t_dst[own_group] = t_src[...]
     tl_dst[own_group] = tl_src[...]
 

time: 42.9 us -> 42.9 us (level)
  no operation moved by 1% of the time
where the time goes in v5:
time: 42.9 us; the launch traced here: 42.8 us
  Pallas kernels  42.1 us (98%)
  between operations  0.65 us (2%)
    pallas_call x1, Pallas kernels, on_device(): pl.pallas_call(functools.partial(main_kernel, n_seq, n_head, n_z), out_sh...  41 us
    pallas_call x1, Pallas kernels, on_device(): pl.pallas_call(last_kernel, out_shape=results, in_specs=[vmem] * 8, out_s...  1.08 us

profile of v5, /device:TPU:1, one launch (start us, length us, event | category | flops | bytes accessed | tf_op | source)
XLA Modules:
  0.0 42.8 jit_solution(6787848858944205613)
XLA Ops:
  0.6 41.0 %main.1 = (bf16[256,256]{1,0:T(8,128)(2,1)S(1)}, bf16[256,256]{1,0:T(8,128)(2,1)S(1)}, bf16[256,256]{1,0:T(8,128)(2,1)S(1)}, bf16[256,256]{1,0:T(8,128)(2,1)S(1)...) custom-call(f32[2]{0:T(128)} %rate_hbm.1, ...), custom_call_target="tpu_custom_call" | custom-call | tf_op jit(solution)/shard_map/main/pallas_call | solution.py:617
  41.7 1.1 %last.1 = (bf16[256,256]{1,0:T(8,128)(2,1)}, bf16[256,256]{1,0:T(8,128)(2,1)}, bf16[256,256]{1,0:T(8,128)(2,1)}, bf16[256,256]{1,0:T(8,128)(2,1)}, bf16[256,128]...) custom-call(bf16[256,256]{1,0:T(8,128)(2,1)S(1)} %get-tuple-element.16.refs_0_, ...), custom_call_target="tpu_custom_call" | custom-call | tf_op jit(solution)/shard_map/last/pallas_call | solution.py:687
